TPU v7x, 512 devices: a whole 4x4x16 slice. The times are simulated.
512 devices in a mesh: band: 64 (over z, x_lo, core), lev: 8 (over y, x_hi).
Axes of the slice: x: 4 (x_hi: 2, x_lo: 2; x = x_hi * 2 + x_lo), y: 4, z: 16, core: 2. Of those that a mesh axis runs over, the one named last changes fastest.
Arguments:
- air_heat_state: bfloat16 [8, 2, 512, 4096], P('lev', None, 'band'), may hold values from -6 to 6
- mixing_coefficient: bfloat16 [2, 512, 4096], P(None, 'band'), may hold values from 0.049804688 to 0.19921875
- layer_depth_factor: float32 [8], P('lev'), may hold values from 0.3 to 0.8
- weighted_polynomial_table: bfloat16 [512, 320, 641], P('band'), may hold values from -0.5 to 0.5
- wavenumber_to_mode_degree: int32 [320], replicated, may hold values from 0 to 319, each once
Outputs:
- smoothed: bfloat16 [8, 2, 512, 4096], P('lev', None, 'band')
- spectral: float32 [8, 2, 2, 320, 641], P('lev', None, None, 'band')
Inputs may be any that keep to these rules, and one draw needn't show every extreme that they name: wavenumber_to_mode_degree holds every pair row 0 to 319 once; pair row p holds wavenumbers p and 639 - p.
All inputs are finite; a program needn't handle non-finite values.
Results may differ from a plain program's by a relative error of at most 0.009.
Values may be sent and summed in bfloat16 or wider, within the bound.
A program may use at most 128 MiB of HBM per device.

v0:
```python
import math

import jax
import jax.numpy as jnp
from jax import lax
from jax.sharding import PartitionSpec as P

MERIDIAN_STEPS = 1024
K = 640


def padded(cells, sides, width):
    for axis, dim in sides:
        count = lax.axis_size(axis)
        ends = count - 1
        head = lax.slice_in_dim(cells, 0, width, axis=dim)
        tail = lax.slice_in_dim(cells, cells.shape[dim] - width, cells.shape[dim], axis=dim)
        cells = jnp.concatenate(
            [
                lax.ppermute(tail, axis, [(i, (i + 1) % count) for i in range(ends)]),
                cells,
                lax.ppermute(head, axis, [((i + 1) % count, i) for i in range(ends)]),
            ],
            axis=dim,
        )
    return cells


def carried_in(shard, axis, join, neutral):
    count = lax.axis_size(axis)
    place = lax.axis_index(axis)
    ahead = count - 1 - place
    gathered = lax.all_gather(shard.astype(jnp.bfloat16), axis)
    state = jnp.zeros_like(shard) + jnp.asarray(neutral, shard.dtype)

    def one(turn, state):
        source = count - 1 - turn
        return join(state, lax.dynamic_index_in_dim(gathered, source, 0, False).astype(shard.dtype))

    return lax.fori_loop(0, ahead, one, state)


def pair_terms(products, pair_index, columns):
    count_pairs = products.shape[0]
    products = products.reshape(count_pairs, 4, products.shape[1] // 4, columns)
    column_ids = jnp.arange(columns, dtype=jnp.int32)[None, :]
    pair_ids = pair_index[:, None]
    first_part = column_ids < columns - 1 - pair_ids
    parity = jnp.where(first_part, column_ids % 2, (column_ids + pair_ids) % 2)
    signs = (1 - 2 * parity).astype(products.dtype)[:, None, :]
    first_part = first_part[:, None, :]
    return jnp.where(
        first_part, products[:, 0] + signs * products[:, 1], products[:, 2] + signs * products[:, 3]
    )


def batched_product(coeff_rows, table_rows):
    return lax.dot_general(
        coeff_rows, table_rows, (((2,), (0,)), ((0,), (1,))), preferred_element_type=jnp.float32
    )


def add_terms(earlier, later):
    return earlier + later


def on_device(
    air_heat_state,
    mixing_coefficient,
    layer_depth_factor,
    weighted_polynomial_table,
    wavenumber_to_mode_degree,
):
    levels_held_locally, hemisphere_pair, latitude_row_count, longitude_cell_count = (
        air_heat_state.shape
    )
    current_band_index = lax.axis_index("band")
    number_of_bands = lax.axis_size("band")
    half_k = K // 2
    slots = half_k // number_of_bands
    padded_with_nulls = padded(air_heat_state, (("band", 2),), 1)
    physical_space_values = air_heat_state.astype(jnp.float32)
    kappa_field = mixing_coefficient.astype(jnp.float32)
    global_rows = (
        current_band_index * latitude_row_count + jnp.arange(latitude_row_count, dtype=jnp.int32)
    ).astype(jnp.float32)
    centre = jnp.sin((global_rows + 0.5) * (math.pi / MERIDIAN_STEPS))[:, None]
    upper_face = jnp.sin((global_rows + 1.0) * (math.pi / MERIDIAN_STEPS))[:, None]
    lower_face = jnp.sin(global_rows * (math.pi / MERIDIAN_STEPS))[:, None]
    eastward = jnp.roll(physical_space_values, -1, axis=3)
    westward = jnp.roll(physical_space_values, 1, axis=3)
    poleward = padded_with_nulls[:, :, :latitude_row_count].astype(jnp.float32)
    beyond = jnp.where(
        current_band_index == number_of_bands - 1,
        air_heat_state[:, ::-1, -1:],
        padded_with_nulls[:, :, latitude_row_count + 1 :],
    )
    equatorward = jnp.concatenate(
        [padded_with_nulls[:, :, 2 : latitude_row_count + 1], beyond], axis=2
    ).astype(jnp.float32)
    meridional = (
        upper_face * (equatorward - physical_space_values)
        - lower_face * (physical_space_values - poleward)
    ) / centre
    smoothed = (
        physical_space_values
        + kappa_field[None] * (eastward - 2.0 * physical_space_values + westward + meridional)
    ).astype(jnp.bfloat16)
    weighted = layer_depth_factor[:, None, None, None] * smoothed.astype(jnp.float32)
    local_total = jnp.sum(weighted, axis=0)
    below = carried_in(local_total, "lev", add_terms, jnp.zeros_like(local_total))
    from_ground = below[None] + jnp.cumsum(weighted[::-1], axis=0)[::-1]
    geopotential = (from_ground - 0.5 * weighted).astype(jnp.bfloat16)
    grid = jnp.stack([smoothed, geopotential], axis=1)
    flat = grid.reshape(-1, longitude_cell_count)
    scale_factor = 1.0 / math.sqrt(longitude_cell_count)

    def transform(block_start):
        frequency = block_start + jnp.arange(128, dtype=jnp.int32)
        phase = (
            jnp.arange(longitude_cell_count, dtype=jnp.int32)[:, None]
            * frequency[None, :]
            % longitude_cell_count
        )
        angle = phase.astype(jnp.float32) * (2.0 * math.pi / longitude_cell_count)
        table = (jnp.concatenate([jnp.cos(angle), -jnp.sin(angle)], axis=1) * scale_factor).astype(
            jnp.bfloat16
        )
        return jnp.dot(flat, table, preferred_element_type=jnp.float32).astype(jnp.bfloat16)

    blocks = lax.map(transform, jnp.arange(0, K, 128, dtype=jnp.int32))
    real_part = jnp.transpose(blocks[:, :, :128], (1, 0, 2)).reshape(
        levels_held_locally, 2, 2, latitude_row_count, K
    )
    imag_part = jnp.transpose(blocks[:, :, 128:], (1, 0, 2)).reshape(
        levels_held_locally, 2, 2, latitude_row_count, K
    )
    fourier = jnp.stack([real_part, imag_part], axis=2)
    channels = levels_held_locally * 4
    north = fourier[:, :, :, 0].reshape(channels, latitude_row_count, K)
    south = fourier[:, :, :, 1].reshape(channels, latitude_row_count, K)
    stacked = jnp.stack(
        [
            north[..., :half_k],
            south[..., :half_k],
            north[..., ::-1][..., :half_k],
            south[..., ::-1][..., :half_k],
        ],
        axis=0,
    )
    arranged = jnp.transpose(stacked, (3, 0, 1, 2)).reshape(
        half_k, 4 * channels, latitude_row_count
    )
    own_pairs = lax.dynamic_slice_in_dim(
        wavenumber_to_mode_degree, current_band_index * slots, slots
    )

    def whole_block(block_start):
        coeff_block = lax.dynamic_slice_in_dim(arranged, block_start, 32, 0)
        table_block = lax.dynamic_slice_in_dim(weighted_polynomial_table, block_start, 32, 1)
        products = batched_product(coeff_block, table_block)
        return pair_terms(products, block_start + jnp.arange(32, dtype=jnp.int32), K + 1)

    partial_sums = lax.map(whole_block, jnp.arange(0, half_k, 32, dtype=jnp.int32)).reshape(
        half_k, channels, K + 1
    )
    summed = lax.psum(partial_sums, "band")
    mine = jnp.take(summed, own_pairs, axis=0)
    spectral = jnp.transpose(mine.reshape(slots, levels_held_locally, 2, 2, K + 1), (1, 2, 3, 0, 4))
    return (smoothed, spectral)


def solution(mesh):
    placed = (
        P("lev", None, "band", None),
        P(None, "band", None),
        P("lev"),
        P("band", None, None),
        P(),
    )
    return jax.shard_map(
        on_device,
        mesh=mesh,
        in_specs=placed,
        out_specs=(P("lev", None, "band", None), P("lev", None, None, "band", None)),
        check_vma=False,
    )
```

profile of v0, /device:TPU:1, one launch (start us, length us, event | category | flops | bytes accessed | tf_op | source)
XLA Modules:
  0.0 664.0 jit_solution(10106278501876686482)
XLA Ops:
  7.2 1.0 fusion.52
  8.2 8.8 %collective-permute-start = (bf16[1,2,1,4096]{3,2,1,0:T(2,128)(2,1)S(1)}, bf16[1,2,1,4096]{3,2,1,0:T(2,128)(2,1)S(1)}, u32[]{:S(2)}, u32[]{:S(2)}) collective-permute-start(bf16[1,2,1,4096]{3,2,1,0:T(2,128)(2,1)S(1)} %get-tuple-element.238), channel_id=1, source_target_pairs={{8,0},{16,8},{24,16},{32,24},{40,32},{48,40},{56,48},{64,56},{72,6... | collective-permute-start | bytes 49160 | tf_op jit(solution)/shard_map/ppermute | solution.py:22
  17.0 1.9 collective-permute-start.1
  19.0 1.1 fusion.50
  20.1 0.8 fusion.51
  20.9 0.9 slice.87
  22.6 2.0 fusion.47
  24.7 60.7 %all-gather.2.cloned.1.call-done = bf16[8,2,8,4096]{3,2,1,0:T(8,128)(2,1)} async-done(((bf16[1,2,8,4096]{3,2,1,0:T(8,128)(2,1)}), bf16[8,2,8,4096]{3,2,1,0:T(8,128)(2,1)}) %all-gather.2.cloned.1.call-update) | async-done | bytes 1048592 | tf_op jit(solution)/shard_map/all_gather | solution.py:33
  85.4 6.8 %while.36 = (s32[]{:T(128)}, f32[2,8,4096]{2,1,0:T(8,128)S(1)}, s32[]{:T(128)}, bf16[8,2,8,4096]{3,2,1,0:T(8,128)(2,1)}, s32[]{:T(128)}, /*index=5*/s32[]{:T(128)}, s32[]{:T(128)}, s32[]{:T(128)}) while((s32[]{:T(128)}, f32[2,8,4096]{2,1,0:T(8,128)S(1)}, s32[]{:T(128)}, bf16[8,2,8,4096]{3,2,1,0:T(8,128)(2,1)}, s32[]{:T(128)}, ...), condition=%wide.region_1.2_spmd, body=%wide.region_0.1_spmd.sunk | while | flops 131078 | bytes 655495 | solution.py:40
  85.4 0.9 convert_add_fusion.2
  86.4 0.9 convert_add_fusion.2
  87.4 0.9 convert_add_fusion.2
  88.4 0.9 convert_add_fusion.2
  89.3 0.9 convert_add_fusion.2
  90.3 0.9 convert_add_fusion.2
  91.3 0.9 convert_add_fusion.2
  92.4 49.9 %while.37 = (s32[]{:T(128)}, bf16[5,32,256]{2,1,0:T(8,128)(2,1)S(1)}, s32[5]{0:T(128)S(1)}, bf16[32,4096]{1,0:T(8,128)(2,1)S(1)}, s32[]{:T(128)}) while((s32[]{:T(128)}, bf16[5,32,256]{2,1,0:T(8,128)(2,1)S(1)}, s32[5]{0:T(128)S(1)}, bf16[32,4096]{1,0:T(8,128)(2,1)S(1)}, s32[]{:T(128)}) %tuple.106), condition=%wide.region_3.4_spmd, body=%wide.region_2.3_spmd.sunk | while | flops 78127232 | bytes 8668241 | solution.py:131
  93.0 0.6 iota_add_fusion.5
  93.6 8.2 %fusion.67 = (f32[4096,128]{1,0:T(8,128)S(1)}, f32[4096,128]{1,0:T(8,128)S(1)}) fusion(s32[128]{0:T(128)S(1)} %iota_add_fusion.5), kind=kLoop, calls=%fused_computation.18.clone.1 | loop fusion | flops 7864320 | bytes 4194816 | tf_op jit(solution)/shard_map/while/body/eval_jaxpr/cos | solution.py:126
  102.3 0.6 dynamic_slice.48
  102.9 0.6 iota_add_fusion.5
  103.6 8.2 %fusion.67 = (f32[4096,128]{1,0:T(8,128)S(1)}, f32[4096,128]{1,0:T(8,128)S(1)}) fusion(s32[128]{0:T(128)S(1)} %iota_add_fusion.5), kind=kLoop, calls=%fused_computation.18.clone.1 | loop fusion | flops 7864320 | bytes 4194816 | tf_op jit(solution)/shard_map/while/body/eval_jaxpr/cos | solution.py:126
  112.3 0.6 dynamic_slice.48
  112.9 0.6 iota_add_fusion.5
  113.6 8.2 %fusion.67 = (f32[4096,128]{1,0:T(8,128)S(1)}, f32[4096,128]{1,0:T(8,128)S(1)}) fusion(s32[128]{0:T(128)S(1)} %iota_add_fusion.5), kind=kLoop, calls=%fused_computation.18.clone.1 | loop fusion | flops 7864320 | bytes 4194816 | tf_op jit(solution)/shard_map/while/body/eval_jaxpr/cos | solution.py:126
  122.9 0.6 iota_add_fusion.5
  123.5 8.2 %fusion.67 = (f32[4096,128]{1,0:T(8,128)S(1)}, f32[4096,128]{1,0:T(8,128)S(1)}) fusion(s32[128]{0:T(128)S(1)} %iota_add_fusion.5), kind=kLoop, calls=%fused_computation.18.clone.1 | loop fusion | flops 7864320 | bytes 4194816 | tf_op jit(solution)/shard_map/while/body/eval_jaxpr/cos | solution.py:126
  132.9 0.6 iota_add_fusion.5
  133.5 8.2 %fusion.67 = (f32[4096,128]{1,0:T(8,128)S(1)}, f32[4096,128]{1,0:T(8,128)S(1)}) fusion(s32[128]{0:T(128)S(1)} %iota_add_fusion.5), kind=kLoop, calls=%fused_computation.18.clone.1 | loop fusion | flops 7864320 | bytes 4194816 | tf_op jit(solution)/shard_map/while/body/eval_jaxpr/cos | solution.py:126
  143.4 67.2 %while.38 = (s32[]{:T(128)}, f32[10,32,4,641]{3,2,1,0:T(4,128)}, s32[10]{0:T(128)S(1)}, bf16[320,16,8]{0,2,1:T(8,128)(2,1)S(1)}, bf16[8,320,641]{2,1,0:T(8,128)(2,1)}, /*index=5*/s32[]{:T(128)}, s32[]{:T(128)}, s32[]{:T(128)}) while((s32[]{:T(128)}, f32[10,32,4,641]{3,2,1,0:T(4,128)}, s32[10]{0:T(128)S(1)}, bf16[320,16,8]{0,2,1:T(8,128)(2,1)S(1)}, ...), condition=%wide.region_5.6_spmd, body=%wide.region_4.5_spmd.sunk | while | flops 6034443 | bytes 6881367 | solution.py:164
  146.0 1.1 constant_dynamic-slice_fusion.5
  148.2 0.7 iota_add_fusion.6
  149.1 1.0 fusion.73
  152.7 1.1 constant_dynamic-slice_fusion.5
  154.9 0.7 iota_add_fusion.6
  155.8 1.0 fusion.73
  159.4 1.1 constant_dynamic-slice_fusion.5
  161.7 0.7 iota_add_fusion.6
  162.5 1.1 fusion.73
  166.1 1.1 constant_dynamic-slice_fusion.5
  168.4 0.7 iota_add_fusion.6
  169.3 1.0 fusion.73
  172.8 1.1 constant_dynamic-slice_fusion.5
  175.1 0.7 iota_add_fusion.6
  176.0 1.1 fusion.73
  179.6 1.1 constant_dynamic-slice_fusion.5
  181.8 0.7 iota_add_fusion.6
  182.7 1.0 fusion.73
  186.3 1.1 constant_dynamic-slice_fusion.5
  188.5 0.7 iota_add_fusion.6
  189.4 1.0 fusion.73
  193.0 1.1 constant_dynamic-slice_fusion.5
  195.3 0.7 iota_add_fusion.6
  196.2 1.0 fusion.73
  199.7 1.1 constant_dynamic-slice_fusion.5
  202.0 0.7 iota_add_fusion.6
  202.9 1.0 fusion.73
  206.5 1.1 constant_dynamic-slice_fusion.5
  208.7 0.7 iota_add_fusion.6
  209.6 1.0 fusion.73
  210.6 0.8 compare_and_fusion
  211.4 442.2 %all-reduce.2.cloned.1.call-done = f32[320,4,641]{2,1,0:T(4,128)} async-done(((f32[320,4,641]{2,1,0:T(4,128)}), f32[320,4,641]{2,1,0:T(4,128)}) %all-reduce.2.cloned.1.call-update) | async-done | bytes 3281936 | tf_op jit(solution)/shard_map/psum | solution.py:167
  653.7 2.7 gather_fusion
  656.5 0.6 copy.35
  (126 shorter events, 24.7 us)
Async XLA Ops:
  7.2 78.2 %all-gather.2.cloned.1.call-start = ((), (), s32[]{:S(2)}) async-start(), calls=%async_computation | async-start | bytes 1179648 | tf_op jit(solution)/shard_map/all_gather | solution.py:33
  8.2 14.3 %collective-permute-start = (bf16[1,2,1,4096]{3,2,1,0:T(2,128)(2,1)S(1)}, bf16[1,2,1,4096]{3,2,1,0:T(2,128)(2,1)S(1)}, u32[]{:S(2)}, u32[]{:S(2)}) collective-permute-start(bf16[1,2,1,4096]{3,2,1,0:T(2,128)(2,1)S(1)} %get-tuple-element.238), channel_id=1, source_target_pairs={{8,0},{16,8},{24,16},{32,24},{40,32},{48,40},{56,48},{64,56},{72,6... | collective-permute-start | bytes 49160 | tf_op jit(solution)/shard_map/ppermute | solution.py:22
  17.0 5.6 collective-permute-start.1
  24.6 67.7 %copy-start = (bf16[1,2,8,4096]{3,2,1,0:T(8,128)(2,1)}, bf16[1,2,8,4096]{3,2,1,0:T(8,128)(2,1)S(1)}, u32[]{:S(2)}) copy-start(bf16[1,2,8,4096]{3,2,1,0:T(8,128)(2,1)S(1)} %get-tuple-element.229) | copy-start | bytes 393220
  24.6 629.0 %all-reduce.2.cloned.1.call-start = ((), (), s32[]{:S(2)}) async-start(), calls=%async_computation.1 | async-start | bytes 7864320 | tf_op jit(solution)/shard_map/psum | solution.py:167
Sparse Core Ops, SparseCore 0:
  24.7 60.6 all-gather.1
  210.8 442.8 all-reduce.1
where the time goes:
time: 666 us; the launch traced here: 664 us
  waiting for transfers between devices  503 us (76%)
  other arithmetic  73.2 us (11%)
  local copies, waits for them, and re-layouts  35.2 us (5%)
  loops' own time  20.3 us (3%)
  between operations  14.9 us (2%)
  starting transfers between devices  10.8 us (2%)
    psum x1, waiting for transfers between devices, on_device(): summed = lax.psum(partial_sums, 'band')  442 us
    all_gather x1, waiting for transfers between devices, carried_in(): gathered = lax.all_gather(shard.astype(jnp.bfloat16), axis)  60.7 us
    cos x5, other arithmetic, transform(): jnp.cos(angle)  41.2 us
    another operation x1, loops' own time, on_device(): lax.map(whole_block, jnp.arange(0, half_k, 32, dtype=jnp.int32))  20 us
  transfers between devices with their start and end apart: 4, of which 2 were waited for; matrix products, arithmetic and copies ran while one was open for 1% of the time, Pallas kernels for 0%

commit v1 on v0

v1 whole, which is shorter than its diff:
```python
import math

import jax
import jax.numpy as jnp
import ml_dtypes
import numpy as np
from jax import lax
from jax.experimental import pallas as pl
from jax.experimental.pallas import tpu as pltpu
from jax.sharding import PartitionSpec as P

LON = 4096
HALF = LON // 2
STEPS = 1024
K = 640
HK = K // 2
ROWS = 8
NZ = 16
SLOTS = 5
F32 = jnp.float32
BF16 = jnp.bfloat16
CHUNKS = (
    ((0, 0), (1, 0), (0, 1), (1, 1), (0, 2), (1, 2)),
    ((0, 3), (1, 3), (0, 4), (1, 4), (None, 5)),
)
ZROWS = 32
TILES = sum(len(c) for c in CHUNKS)
ZORDER = (8, 7, 9, 6, 10, 5, 11, 4, 12, 3, 13, 2, 14, 1, 15)


def fourier_table():
    p = np.arange(HK)
    m = np.concatenate([p, K - 1 - p])
    phase = (m[:, None] * np.arange(HALF)[None, :]) % LON
    angle = phase * (2.0 * math.pi / LON)
    table = np.concatenate([np.cos(angle), -np.sin(angle)], axis=0) / math.sqrt(LON)
    return table.astype(ml_dtypes.bfloat16)


def spread_tables():
    out = np.zeros((4, 2, 2, ROWS, ROWS, 128), np.float32)
    lane = np.arange(128)
    for half in range(2):
        for hem in range(2):
            a = np.ones(128) if hem == 0 else 1.0 - 2.0 * (lane % 2)
            b = np.ones(128) if hem == 0 else 1.0 - 2.0 * ((lane + 1 - half) % 2)
            for j in range(ROWS):
                out[0, half, hem, j, j] = a
                out[1, half, hem, j, j] = b
                out[2, half, hem, j, j, 0] = b[0]
                out[3, half, hem, j, j, 1] = b[0]
    return out.reshape(4 * 4 * ROWS, ROWS * 128).astype(ml_dtypes.bfloat16)


def nt(a, b):
    return lax.dot_general(a, b, (((1,), (1,)), ((), ())), preferred_element_type=F32)


def kernel(
    air, kappa, before, after, thick, perm, w_hbm, e_hbm, t_hbm,
    smooth, spectral,
    w, e, t, x, onehot, coef_a, coef_b, coef_x, partial,
    core_send, core_recv, own, x_send, x_recv, summed, packed, z_send, z_recv,
    field, lev_send, lev_recv,
    in_sem, core_sem, x_sem, zs_sem, zr_sem, ls_sem, lr_sem,
):
    band = lax.axis_index("band")
    lev = lax.axis_index("lev")
    z, xlo, core = band // 4, (band // 2) % 2, band % 2

    def at(zz, xx, cc, ll):
        return ((zz * 2 + xx) * 2 + cc, ll)

    core_peer = at(z, xlo, 1 - core, lev)
    x_peer = at(z, 1 - xlo, core, lev)
    z_peer = {d: at((z + d) % NZ, xlo, core, lev) for d in range(1, NZ)}
    lev_peer = {d: at(z, xlo, core, (lev + 8 - d) % 8) for d in range(1, 8)}
    mesh_id = pl.DeviceIdType.MESH

    barrier = pltpu.get_barrier_semaphore()
    peers = [core_peer, x_peer, *z_peer.values(), *lev_peer.values()]
    for peer in peers:
        pl.semaphore_signal(barrier, inc=1, device_id=peer, device_id_type=mesh_id)

    loads = [
        pltpu.make_async_copy(
            w_hbm.at[pl.ds(k * HK, HK)], w.at[pl.ds(k * HK, HK)], in_sem.at[k]
        )
        for k in range(4)
    ]
    loads.append(pltpu.make_async_copy(e_hbm, e, in_sem.at[4]))
    loads.append(pltpu.make_async_copy(t_hbm, t, in_sem.at[5]))
    for load in loads:
        load.start()

    row = lax.broadcasted_iota(jnp.int32, (ROWS, 1), 0)
    j = (band * ROWS + row).astype(F32)
    step = math.pi / STEPS
    centre = jnp.sin((j + 0.5) * step)
    upper = jnp.sin((j + 1.0) * step) / centre
    lower = jnp.sin(j * step) / centre
    last = band == 63
    folded = []
    for hem in range(2):
        u = air[0, hem].astype(F32)
        kap = kappa[hem].astype(F32)
        pole = before[hem : hem + 1, :].astype(F32)
        across = air[0, 1 - hem].astype(F32)[ROWS - 1 :, :]
        beyond = jnp.where(last, across, after[hem : hem + 1, :].astype(F32))
        prev = jnp.where(row == 0, pole, pltpu.roll(u, 1, 0))
        succ = jnp.where(row == ROWS - 1, beyond, pltpu.roll(u, ROWS - 1, 0))
        east = pltpu.roll(u, LON - 1, 1)
        west = pltpu.roll(u, 1, 1)
        s = u + kap * (east - 2.0 * u + west + upper * (succ - u) - lower * (u - prev))
        s = s.astype(BF16)
        smooth[0, hem] = s
        s = s.astype(F32)
        folded.append((s[:, :HALF] + s[:, HALF:], s[:, :HALF] - s[:, HALF:]))
    for half in range(2):
        x[pl.ds(16 * half, 16), :] = jnp.concatenate(
            [folded[0][half], folded[1][half]], axis=0
        ).astype(BF16)

    r = lax.broadcasted_iota(jnp.int32, (HK, HK), 0)
    col = lax.broadcasted_iota(jnp.int32, (HK, HK), 1)
    group = (r * 205) >> 10
    dz, dx, dc = group & 15, (group >> 4) & 1, group >> 5
    to_x = jnp.where(dx == 0, 1 - xlo, xlo)
    to_c = jnp.where(dc == 0, 1 - core, core)
    slot = ((((z + dz) & 15) * 2 + to_x) * 2 + to_c) * SLOTS + (r - 5 * group)
    order = jnp.where(slot == col, 1.0, 0.0).astype(BF16)
    pair_of = jnp.where(r == perm[...], 1.0, 0.0).astype(BF16)
    onehot[...] = nt(order, pair_of).astype(BF16)

    pairs = lax.broadcasted_iota(jnp.int32, (HK, 32), 0)
    lanes = lax.broadcasted_iota(jnp.int32, (HK, 32), 1)
    loads[4].wait()
    xs = x[...]
    for k in range(4):
        loads[k].wait()
        sums = nt(w[pl.ds(k * HK, HK), :], xs)
        part, back = k // 2, k % 2
        keep = (lanes < 16) == ((pairs + back) % 2 == 0)
        f = jnp.where(keep, sums, 0.0).astype(BF16)
        target = coef_b if back else coef_a
        target[part] = jnp.dot(
            f, e[pl.ds(32 * back, 32), :], preferred_element_type=F32
        )
        if back:
            c = jnp.dot(
                f, e[pl.ds(64 + 32 * part, 32), :], preferred_element_type=F32
            )
            if part == 0:
                coef_x[...] = c
            else:
                coef_x[...] += c
    loads[5].wait()

    def legendre(q, first, count, kind):
        lane = lax.broadcasted_iota(jnp.int32, (16, 128), 1)
        sub = lax.broadcasted_iota(jnp.int32, (16, 128), 0)

        def body(i, carry):
            p0 = pl.multiple_of((first + i) * 16, 16)
            acc = [jnp.zeros((16, 128), F32) for _ in range(2)]
            if kind == "ab":
                front = 128 * q + lane < K - p0 - sub
            for jj in range(ROWS):
                tt = t[jj, pl.ds(p0, 16), 128 * q : 128 * q + 128].astype(F32)
                for part in range(2):
                    where = (part, pl.ds(p0, 16), pl.ds(128 * jj, 128))
                    if kind == "a":
                        c = coef_a[where]
                    elif kind == "b":
                        c = coef_b[where]
                    else:
                        c = jnp.where(front, coef_a[where], coef_b[where])
                    acc[part] = acc[part] + c * tt
            for part in range(2):
                place = 128 * (2 * q + part)
                partial[pl.ds(p0, 16), place : place + 128] = acc[part].astype(BF16)
            return carry

        lax.fori_loop(0, count, body, 0)

    def legendre_last():
        def body(i, carry):
            p0 = pl.multiple_of(i * 16, 16)
            acc = jnp.zeros((16, 128), F32)
            for jj in range(ROWS):
                tt = t[jj, pl.ds(p0, 16), K : K + 1].astype(F32)
                acc = acc + coef_x[pl.ds(p0, 16), pl.ds(128 * jj, 128)] * tt
            partial[pl.ds(p0, 16), 10 * 128 :] = acc.astype(BF16)
            return carry

        lax.fori_loop(0, HK // 16, body, 0)

    def sums_of(q):
        full = min(max((K - 127 - 128 * q) // 16, 0), HK // 16)
        none = min((K - 128 * q) // 16, HK // 16)
        for lo, hi, kind in (
            (0, full, "a"),
            (full, none, "ab"),
            (none, HK // 16, "b"),
        ):
            if hi > lo:
                legendre(q, lo, hi - lo, kind)

    core_copy, x_copy, z_copy = {}, {}, {}
    offset = (0, 128 * len(CHUNKS[0]))

    def core_step(c):
        n = 128 * len(CHUNKS[c])
        cols = slice(offset[c], offset[c] + n)
        mine = partial[:, cols]
        core_send[:, cols] = jnp.dot(
            onehot[pl.ds(0, 160), :], mine, preferred_element_type=F32
        ).astype(BF16)
        core_copy[c] = pltpu.make_async_remote_copy(
            src_ref=core_send.at[:, cols],
            dst_ref=core_recv.at[:, cols],
            send_sem=core_sem.at[0, c],
            recv_sem=core_sem.at[1, c],
            device_id=core_peer,
            device_id_type=mesh_id,
        )
        if c == 0:
            pl.semaphore_wait(barrier, len(peers))
        core_copy[c].start()
        own[:, cols] = jnp.dot(
            onehot[pl.ds(160, 160), :], mine, preferred_element_type=F32
        )

    def x_step(c):
        n = 128 * len(CHUNKS[c])
        cols = slice(offset[c], offset[c] + n)
        core_copy[c].wait_recv()
        x_send[:, cols] = (
            own[pl.ds(0, 80), cols] + core_recv[pl.ds(0, 80), cols].astype(F32)
        ).astype(BF16)
        x_copy[c] = pltpu.make_async_remote_copy(
            src_ref=x_send.at[:, cols],
            dst_ref=x_recv.at[:, cols],
            send_sem=x_sem.at[0, c],
            recv_sem=x_sem.at[1, c],
            device_id=x_peer,
            device_id_type=mesh_id,
        )
        x_copy[c].start()

    def z_step(c):
        n = 128 * len(CHUNKS[c])
        cols = slice(offset[c], offset[c] + n)
        x_copy[c].wait_recv()
        summed[:, cols] = (
            own[pl.ds(80, 80), cols]
            + core_recv[pl.ds(80, 80), cols].astype(F32)
            + x_recv[:, cols].astype(F32)
        )
        for d in range(NZ):
            for i in range(len(CHUNKS[c])):
                packed[c, d, 5 * i : 5 * i + 5, :] = summed[
                    5 * d : 5 * d + 5, offset[c] + 128 * i : offset[c] + 128 * i + 128
                ]
        for d in range(1, NZ):
            z_send[c, d] = packed[c, d].astype(BF16)
        z_copy[c] = []
        for d in ZORDER:
            copy = pltpu.make_async_remote_copy(
                src_ref=z_send.at[c, d],
                dst_ref=z_recv.at[c, d],
                send_sem=zs_sem.at[c, d],
                recv_sem=zr_sem.at[c, d],
                device_id=z_peer[d],
                device_id_type=mesh_id,
            )
            copy.start()
            z_copy[c].append(copy)

    packed[...] = jnp.zeros_like(packed)
    sums_of(0)
    sums_of(1)
    sums_of(2)
    core_step(0)
    sums_of(3)
    x_step(0)
    sums_of(4)
    legendre_last()
    core_step(1)
    x_step(1)
    z_step(0)
    z_step(1)

    thickness = thick[0]
    for c in range(len(CHUNKS)):
        for copy in z_copy[c]:
            copy.wait_recv()
        total = packed[c, 0]
        for d in range(1, NZ):
            total = total + z_recv[c, d].astype(F32)
        field[0, pl.ds(ZROWS * c, ZROWS), :] = total
        lev_send[pl.ds(ZROWS * c, ZROWS), :] = (total * thickness).astype(BF16)
    lev_copy = {
        d: pltpu.make_async_remote_copy(
            src_ref=lev_send,
            dst_ref=lev_recv.at[d],
            send_sem=ls_sem.at[d],
            recv_sem=lr_sem.at[d],
            device_id=lev_peer[d],
            device_id_type=mesh_id,
        )
        for d in range(1, 8)
    }
    for d in range(7, 0, -1):

        @pl.when(lev >= d)
        def _():
            lev_copy[d].start()

    field[1] = (0.5 * thickness) * field[0]

    def put(f):
        for c, tiles in enumerate(CHUNKS):
            for n, (part, q) in enumerate(tiles):
                for i in range(SLOTS):
                    k = ZROWS * c + 5 * n + i
                    if part is None:
                        for half in range(2):
                            spectral[f, i, half : half + 1, K : K + 1] = field[
                                f, k : k + 1, half : half + 1
                            ]
                    else:
                        spectral[f, i, part : part + 1, 128 * q : 128 * q + 128] = (
                            field[f, k : k + 1, :]
                        )

    put(0)
    for d in range(1, 8):

        @pl.when(lev + d < 8)
        def _():
            lev_copy[d].wait_recv()
            field[1] += lev_recv[d].astype(F32)

    put(1)

    for c in range(len(CHUNKS)):
        core_copy[c].wait_send()
        x_copy[c].wait_send()
        for copy in z_copy[c]:
            copy.wait_send()
    for d in range(1, 8):

        @pl.when(lev >= d)
        def _():
            lev_copy[d].wait_send()


def on_device(air, kappa, thick, table, perm):
    tail = air[0, :, ROWS - 1, :]
    head = air[0, :, 0, :]
    before = lax.ppermute(tail, "band", [(i, i + 1) for i in range(63)])
    after = lax.ppermute(head, "band", [(i + 1, i) for i in range(63)])
    vmem = pl.BlockSpec(memory_space=pltpu.VMEM)
    hbm = pl.BlockSpec(memory_space=pl.ANY)
    nc = len(CHUNKS)
    wide = 128 * TILES
    smooth, spectral = pl.pallas_call(
        kernel,
        out_shape=(
            jax.ShapeDtypeStruct((1, 2, ROWS, LON), BF16),
            jax.ShapeDtypeStruct((2, SLOTS, 2, K + 1), F32),
        ),
        in_specs=[
            vmem, vmem, vmem, vmem, pl.BlockSpec(memory_space=pltpu.SMEM), vmem,
            hbm, hbm, hbm,
        ],
        out_specs=(vmem, vmem),
        scratch_shapes=[
            pltpu.VMEM((4 * HK, HALF), BF16),
            pltpu.VMEM((128, ROWS * 128), BF16),
            pltpu.VMEM((ROWS, HK, K + 1), BF16),
            pltpu.VMEM((32, HALF), BF16),
            pltpu.VMEM((HK, HK), BF16),
            pltpu.VMEM((2, HK, ROWS * 128), F32),
            pltpu.VMEM((2, HK, ROWS * 128), F32),
            pltpu.VMEM((HK, ROWS * 128), F32),
            pltpu.VMEM((HK, wide), BF16),
            pltpu.VMEM((160, wide), BF16),
            pltpu.VMEM((160, wide), BF16),
            pltpu.VMEM((160, wide), F32),
            pltpu.VMEM((80, wide), BF16),
            pltpu.VMEM((80, wide), BF16),
            pltpu.VMEM((80, wide), F32),
            pltpu.VMEM((nc, NZ, ZROWS, 128), F32),
            pltpu.VMEM((nc, NZ, ZROWS, 128), BF16),
            pltpu.VMEM((nc, NZ, ZROWS, 128), BF16),
            pltpu.VMEM((2, nc * ZROWS, 128), F32),
            pltpu.VMEM((nc * ZROWS, 128), BF16),
            pltpu.VMEM((8, nc * ZROWS, 128), BF16),
            pltpu.SemaphoreType.DMA((6,)),
            pltpu.SemaphoreType.DMA((2, nc)),
            pltpu.SemaphoreType.DMA((2, nc)),
            pltpu.SemaphoreType.DMA((nc, NZ)),
            pltpu.SemaphoreType.DMA((nc, NZ)),
            pltpu.SemaphoreType.DMA((8,)),
            pltpu.SemaphoreType.DMA((8,)),
        ],
        compiler_params=pltpu.CompilerParams(
            collective_id=0, has_side_effects=True, vmem_limit_bytes=56 * 2**20
        ),
        name="transform",
    )(
        air,
        kappa,
        before,
        after,
        thick,
        perm.reshape(1, HK),
        jnp.asarray(fourier_table()),
        jnp.asarray(spread_tables()),
        table,
    )
    return smooth, jnp.transpose(spectral, (0, 2, 1, 3))[None]


def solution(mesh):
    return jax.shard_map(
        on_device,
        mesh=mesh,
        in_specs=(
            P("lev", None, "band", None),
            P(None, "band", None),
            P("lev"),
            P("band", None, None),
            P(),
        ),
        out_specs=(P("lev", None, "band", None), P("lev", None, None, "band", None)),
        check_vma=False,
    )
```

time: 666 us -> 63.5 us (0.10)
  waiting for transfers between devices: 503 us -> 0.01 us
  other arithmetic: 73.2 us -> 0 us
  Pallas kernels: 0 us -> 45 us
  local copies, waits for them, and re-layouts: 35.2 us -> 6.6 us
  loops' own time: 20.3 us -> 0 us
  between operations: 14.9 us -> 1.32 us
    psum x1 -> x0, waiting for transfers between devices: 442 us -> none  [on_device(): summed = lax.psum(partial_sums, 'band')]
    all_gather x1 -> x0, waiting for transfers between devices: 60.7 us -> none  [carried_in(): gathered = lax.all_gather(shard.astype(jnp.bfloat16), axis)]
    pallas_call x0 -> x1, Pallas kernels: none -> 45 us  [on_device(): pl.pallas_call(kernel, out_shape=(jax.ShapeDtypeStruct((1, 2, ROWS, LON),...]
    cos x5 -> x0, other arithmetic: 41.2 us -> none  [transform(): jnp.cos(angle)]
    dynamic_slice x45 -> x0, local copies, waits for them, and re-layouts: 22.3 us -> none  [the longest x10 11.4 us: whole_block(): lax.dynamic_slice_in_dim(weighted_polynomial_table, block_start, 32, 1)]
    another operation x3 -> x0, loops' own time: 20.3 us -> none  [the longest x1 20 us: on_device(): lax.map(whole_block, jnp.arange(0, half_k, 32, dtype=jnp.int32))]
    add x22 -> x0, other arithmetic: 16.4 us -> none  [the longest x7 6.63 us: add_terms(): return earlier + later]
    dynamic_update_slice x10 -> x0, other arithmetic: 10.4 us -> none  [on_device(): lax.map(whole_block, jnp.arange(0, half_k, 32, dtype=jnp.int32))]
  transfers between devices with their start and end apart: 4 -> 2, of which waited for: 2 -> 0; matrix products, arithmetic and copies ran while one was open for 1% -> 2% of each run, Pallas kernels for 0% -> 0%
where the time goes in v1:
time: 63.5 us; the launch traced here: 63 us
  Pallas kernels  45 us (71%)
  starting transfers between devices  10.1 us (16%)
  local copies, waits for them, and re-layouts  6.6 us (10%)
  between operations  1.32 us (2%)
    pallas_call x1, Pallas kernels, on_device(): pl.pallas_call(kernel, out_shape=(jax.ShapeDtypeStruct((1, 2, ROWS, LON),...  45 us
    ppermute x1, starting transfers between devices, on_device(): after = lax.ppermute(head, 'band', [(i + 1, i) for i in range(63)])  5.57 us
    ppermute x1, starting transfers between devices, on_device(): before = lax.ppermute(tail, 'band', [(i, i + 1) for i in range(63)])  4.51 us
    unnamed x8, local copies, waits for them, and re-layouts  4.29 us
    reshape x1, local copies, waits for them, and re-layouts, on_device(): perm.reshape(1, HK)  1.28 us
  transfers between devices with their start and end apart: 2, of which 0 were waited for; matrix products, arithmetic and copies ran while one was open for 2% of the time, Pallas kernels for 0%

profile of v1, /device:TPU:1, one launch (start us, length us, event | category | flops | bytes accessed | tf_op | source)
XLA Modules:
  0.0 63.0 jit_solution(6185869513211388260)
XLA Ops:
  0.6 1.0 %fusion = (bf16[1,2,1,4096]{3,2,1,0:T(2,128)(2,1)S(1)}, bf16[1,2,1,4096]{3,2,1,0:T(2,128)(2,1)S(1)}) fusion(bf16[1,2,8,4096]{3,2,1,0:T(8,128)(2,1)} %air.1), kind=kLoop, calls=%fused_computation.2 | loop fusion | bytes 65536 | tf_op jit(solution)/shard_map/slice | solution.py:361
  1.7 4.5 %collective-permute-start = (bf16[2,4096]{1,0:T(2,128)(2,1)S(1)}, bf16[2,4096]{1,0:T(2,128)(2,1)S(1)}, u32[]{:S(2)}, u32[]{:S(2)}) collective-permute-start(bf16[2,4096]{1,0:T(2,128)(2,1)S(1)} %bitcast.10), channel_id=1, source_target_pairs={{0,8},{8,16},{16,24},{24,32},{32,40},{40,48},{48,56},{56,64},{64,7... | collective-permute-start | bytes 49160 | tf_op jit(solution)/shard_map/ppermute | solution.py:362
  6.3 5.6 %collective-permute-start.1 = (bf16[2,4096]{1,0:T(2,128)(2,1)S(1)}, bf16[2,4096]{1,0:T(2,128)(2,1)S(1)}, u32[]{:S(2)}, u32[]{:S(2)}) collective-permute-start(bf16[2,4096]{1,0:T(2,128)(2,1)S(1)} %bitcast.11), channel_id=1, source_target_pairs={{8,0},{16,8},{24,16},{32,24},{40,32},{48,40},{56,48},{64,56},{72,6... | collective-permute-start | bytes 49160 | tf_op jit(solution)/shard_map/ppermute | solution.py:363
  12.5 1.3 %reshape.7.perm = s32[1,320]{1,0:T(1,128)} reshape(s32[320]{0:T(512)} %param.11) | data formatting | bytes 2560 | tf_op jit(solution)/shard_map/reshape | solution.py:419
  13.8 0.0 collective-permute-done.before
  13.8 0.0 copy-start
  13.8 0.0 collective-permute-done.1.after
  13.8 0.6 copy-done
  14.4 0.0 copy-start.1
  14.4 0.6 copy-done.1
  15.0 45.0 %transform.1 = (bf16[1,2,8,4096]{3,2,1,0:T(8,128)(2,1)}, f32[2,5,2,641]{3,2,1,0:T(2,128)}) custom-call(bf16[1,2,8,4096]{3,2,1,0:T(8,128)(2,1)} %air.1, bf16[2,8,4096]{2,1,0:T(8,128)(2,1)} %kappa.1, bf16[2,4096]{1,0:T(2,128)(2,1)} %copy-done, bf16[2,4096]{1,0:T(2,128)(2,1)} %copy-done.1, f32[1]{0:T(128)S(6)} %copy.19.thick, s32[1,320]{1,0:T(1,128)} %reshape.7.perm, ...), custom_call_target="tpu_custom_call" | custom-call | tf_op jit(solution)/shard_map/transform/pallas_call | solution.py:368
  60.0 1.6 %copy.20 = bf16[1,2,8,4096]{3,2,1,0:T(8,128)(2,1)} copy(bf16[1,2,8,4096]{3,2,1,0:T(8,128)(2,1)} %get-tuple-element.10) | data formatting | bytes 262144
  61.6 1.5 %copy.21 = f32[1,2,2,5,641]{4,2,3,1,0:T(2,128)} copy(f32[1,2,2,5,641]{4,2,3,1,0:T(2,128)} %bitcast.9) | data formatting | bytes 102560
  (2 shorter events, 0.1 us)
Async XLA Ops:
  1.7 12.1 %collective-permute-start = (bf16[2,4096]{1,0:T(2,128)(2,1)S(1)}, bf16[2,4096]{1,0:T(2,128)(2,1)S(1)}, u32[]{:S(2)}, u32[]{:S(2)}) collective-permute-start(bf16[2,4096]{1,0:T(2,128)(2,1)S(1)} %bitcast.10), channel_id=1, source_target_pairs={{0,8},{8,16},{16,24},{24,32},{32,40},{40,48},{48,56},{56,64},{64,7... | collective-permute-start | bytes 49160 | tf_op jit(solution)/shard_map/ppermute | solution.py:362
  6.3 7.5 %collective-permute-start.1 = (bf16[2,4096]{1,0:T(2,128)(2,1)S(1)}, bf16[2,4096]{1,0:T(2,128)(2,1)S(1)}, u32[]{:S(2)}, u32[]{:S(2)}) collective-permute-start(bf16[2,4096]{1,0:T(2,128)(2,1)S(1)} %bitcast.11), channel_id=1, source_target_pairs={{8,0},{16,8},{24,16},{32,24},{40,32},{48,40},{56,48},{64,56},{72,6... | collective-permute-start | bytes 49160 | tf_op jit(solution)/shard_map/ppermute | solution.py:363
  13.8 0.6 copy-start
  14.4 0.6 copy-start.1

commit v2 on v1

v2 whole, which is shorter than its diff:
```python
import math

import jax
import jax.numpy as jnp
import ml_dtypes
import numpy as np
from jax import lax
from jax.experimental import pallas as pl
from jax.experimental.pallas import tpu as pltpu
from jax.sharding import PartitionSpec as P

LON = 4096
FOLD = 4
WAVE = LON // FOLD
STEPS = 1024
K = 640
HK = K // 2
ROWS = 8
NZ = 16
SLOTS = 5
F32 = jnp.float32
BF16 = jnp.bfloat16
CHUNKS = (
    ((0, 0), (1, 0), (0, 1)),
    ((1, 1), (0, 2), (1, 2)),
    ((0, 3), (1, 3)),
    ((0, 4), (1, 4), (None, 5)),
)
PLACE = {tile: k for k, tile in enumerate(t for c in CHUNKS for t in c)}
START = tuple(128 * PLACE[c[0]] for c in CHUNKS)
ZROWS = 16
TILES = len(PLACE)
LAST = (0, 2)
ZORDER = (8, 7, 9, 6, 10, 5, 11, 4, 12, 3, 13, 2, 14, 1, 15)


def fourier_table():
    p = np.arange(HK)
    m = np.concatenate([p, K - 1 - p])
    angle = (m[:, None] * np.arange(WAVE)[None, :] % LON) * (2.0 * math.pi / LON)
    table = np.concatenate([np.cos(angle), -np.sin(angle)], axis=0) / math.sqrt(LON)
    return table.astype(ml_dtypes.bfloat16)


def spread_tables():
    out = np.zeros((2, 4, 2, ROWS, ROWS, 128), np.float32)
    lane = np.arange(128)
    for group in range(4):
        odd_pair = 1 if group < 2 else 0
        for j in range(ROWS):
            out[:, group, 0, j, j] = 1.0
            out[0, group, 1, j, j] = 1.0 - 2.0 * (lane % 2)
            out[1, group, 1, j, j] = 1.0 - 2.0 * ((lane + odd_pair) % 2)
    return out.reshape(2 * 8 * ROWS, ROWS * 128).astype(ml_dtypes.bfloat16)


def nt(a, b):
    return lax.dot_general(a, b, (((1,), (1,)), ((), ())), preferred_element_type=F32)


def kernel(
    air_hbm, kappa_hbm, thick, perm_hbm, w_hbm, e_hbm, t_hbm,
    smooth_hbm, field,
    air, kappa, perm, smooth,
    halo_rows, halo_send, halo_recv, base, x_base, w, e, t, xc, xs, onehot, coef_a, coef_b, partial,
    core_send, core_recv, own, x_send, x_recv, summed, packed, z_send, z_recv,
    lev_send, lev_recv,
    in_sem, out_sem, halo_sem, core_sem, x_sem, zs_sem, zr_sem, ls_sem, lr_sem, told,
):
    band = lax.axis_index("band")
    lev = lax.axis_index("lev")
    z, xlo, core = band // 4, (band // 2) % 2, band % 2

    def at(zz, xx, cc, ll):
        return ((zz * 2 + xx) * 2 + cc, ll)

    yy, xhi = lev // 2, lev % 2
    core_peer = at(z, xlo, 1 - core, lev)
    x_peer = at(z, 1 - xlo, core, lev)
    z_peer = {d: at((z + d) % NZ, xlo, core, lev) for d in range(1, NZ)}
    lev_peer = {d: at(z, xlo, core, (lev + 8 - d) % 8) for d in range(1, 8)}
    y_peer = {d: at(z, xlo, core, ((yy + d) % 4) * 2 + xhi) for d in (1, 3)}
    far_x_peer = at(z, xlo, core, yy * 2 + 1 - xhi)
    halo_peer = (((band + 1) % 64, lev), ((band + 63) % 64, lev))
    mesh_id = pl.DeviceIdType.MESH

    barrier = pltpu.get_barrier_semaphore()
    peers = [
        *halo_peer, x_peer, z_peer[1], z_peer[15], y_peer[1], y_peer[3], far_x_peer,
    ]
    for peer in peers:
        pl.semaphore_signal(barrier, inc=1, device_id=peer, device_id_type=mesh_id)

    def tell(k, peer):
        pl.semaphore_signal(
            told.at[k], inc=1, device_id=peer, device_id_type=mesh_id
        )

    def heard(*ks):
        for k in ks:
            pl.semaphore_wait(told.at[k], 1)

    loads = [
        pltpu.make_async_copy(src, dst, in_sem.at[n])
        for n, (src, dst) in enumerate(
            [(air_hbm, air), (kappa_hbm, kappa), (perm_hbm, perm)]
            + [
                (w_hbm.at[pl.ds(k * HK, HK)], w.at[pl.ds(k * HK, HK)])
                for k in (0, 2, 1, 3)
            ]
            + [(e_hbm, e)]
            + [(t_hbm.at[k], t.at[k]) for k in range(ROWS)]
        )
    ]
    for load in loads:
        load.start()
    packed[...] = jnp.zeros_like(packed)

    row = lax.broadcasted_iota(jnp.int32, (ROWS, 1), 0)
    loads[0].wait()
    for hem in range(2):
        base[hem] = air[0, hem].astype(F32)
    for way, r in enumerate((ROWS - 1, 0)):
        for hem in range(2):
            for k in range(8):
                halo_rows[way, 8 * hem + k : 8 * hem + k + 1, :] = base[
                    hem, r : r + 1, 512 * k : 512 * k + 512
                ]
        halo_send[way] = halo_rows[way].astype(BF16)
    pl.semaphore_wait(barrier, len(peers))
    halo_copy = [
        pltpu.make_async_remote_copy(
            src_ref=halo_send.at[way],
            dst_ref=halo_recv.at[way],
            send_sem=halo_sem.at[0, way],
            recv_sem=halo_sem.at[1, way],
            device_id=halo_peer[way],
            device_id_type=mesh_id,
        )
        for way in range(2)
    ]
    for copy in halo_copy:
        copy.start()
    tell(0, z_peer[1])
    tell(1, z_peer[15])
    tell(6, y_peer[1])
    tell(7, y_peer[3])
    j = (band * ROWS + row).astype(F32)
    step = math.pi / STEPS
    centre = jnp.sin((j + 0.5) * step)
    upper = jnp.sin((j + 1.0) * step) / centre
    lower = jnp.sin(j * step) / centre
    last = band == 63
    loads[1].wait()
    for hem in range(2):
        u = base[hem]
        across = base[1 - hem][ROWS - 1 :, :]
        prev = jnp.where(row == 0, 0.0, pltpu.roll(u, 1, 0))
        succ = jnp.where(
            row == ROWS - 1, jnp.where(last, across, 0.0), pltpu.roll(u, ROWS - 1, 0)
        )
        east = pltpu.roll(u, LON - 1, 1)
        west = pltpu.roll(u, 1, 1)
        merid = upper * (succ - u) - lower * (u - prev)
        x_base[hem] = u + kappa[hem].astype(F32) * (east - 2.0 * u + west + merid)

    loads[2].wait()
    r = lax.broadcasted_iota(jnp.int32, (HK, HK), 0)
    col = lax.broadcasted_iota(jnp.int32, (HK, HK), 1)
    group = (r * 205) >> 10
    dz, dx, dc = group & 15, (group >> 4) & 1, group >> 5
    to_x = jnp.where(dx == 0, 1 - xlo, xlo)
    to_c = jnp.where(dc == 0, 1 - core, core)
    slot = ((((z + dz) & 15) * 2 + to_x) * 2 + to_c) * SLOTS + (r - 5 * group)
    order = jnp.where(slot == col, 1.0, 0.0).astype(BF16)
    pair_of = jnp.where(r == perm[...].reshape(1, HK), 1.0, 0.0).astype(BF16)
    onehot[...] = nt(order, pair_of).astype(BF16)

    heard(0, 1, 6, 7)
    tell(2, z_peer[2])
    tell(3, z_peer[14])
    tell(8, far_x_peer)

    folded = []
    for way in range(2):
        halo_copy[way].wait_recv()
        halo_rows[way] = halo_recv[way].astype(F32)
    for hem in range(2):
        pole, beyond = (
            jnp.concatenate(
                [halo_rows[way, 8 * hem + k : 8 * hem + k + 1, :] for k in range(8)],
                axis=1,
            )
            for way in range(2)
        )
        at_pole = jnp.where((row == 0) & (band > 0), lower, 0.0)
        at_edge = jnp.where((row == ROWS - 1) & (band < 63), upper, 0.0)
        s = x_base[hem] + kappa[hem].astype(F32) * (at_pole * pole + at_edge * beyond)
        s = s.astype(BF16)
        smooth[0, hem] = s
        folded.append(s.astype(F32))
    save = pltpu.make_async_copy(smooth, smooth_hbm, out_sem)
    save.start()
    q0, q1, q2, q3 = (
        jnp.concatenate([s[:, WAVE * k : WAVE * k + WAVE] for s in folded], axis=0)
        for k in range(FOLD)
    )
    even, odd = q0 + q2, q1 + q3
    y0, y2 = (even + odd).astype(BF16), (even - odd).astype(BF16)
    d02, d13 = (q0 - q2).astype(BF16), (q1 - q3).astype(BF16)
    for k, (c, d) in enumerate(((y0, y0), (y2, y2), (d02, d13), (d13, d02))):
        xc[pl.ds(16 * k, 16), :] = c
        xs[pl.ds(16 * k, 16), :] = d

    pairs = lax.broadcasted_iota(jnp.int32, (HK, 64), 0)
    group = lax.broadcasted_iota(jnp.int32, (HK, 64), 1) >> 4
    loads[7].wait()
    for back in range(2):
        m = (K - 1 - pairs if back else pairs) & 3
        loads[3 + 2 * back].wait()
        loads[4 + 2 * back].wait()
        cosine = nt(w[pl.ds(back * HK, HK), :], xc[...])
        sine = nt(w[pl.ds(K + back * HK, HK), :], xs[...])
        target = coef_b if back else coef_a
        turn = jnp.where(m == 1, 1.0, -1.0)
        real = cosine + jnp.where(group == 2, turn * sine, 0.0)
        imag = sine - jnp.where(group == 3, turn * cosine, 0.0)
        odd = (m & 1) == 1
        for part, (f, g) in enumerate(((real, 2), (imag, 3))):
            keep = group == jnp.where(odd, g, m >> 1)
            target[part] = jnp.dot(
                jnp.where(keep, f, 0.0).astype(BF16),
                e[pl.ds(64 * back, 64), :],
                preferred_element_type=F32,
            )
    heard(2, 3, 8)
    tell(4, z_peer[4])
    tell(5, z_peer[12])
    for load in loads[8:]:
        load.wait()

    def kind_of(q, block):
        if q == 5:
            return "x"
        if 16 * block + 15 < K - 127 - 128 * q:
            return "a"
        return "b" if 16 * block >= K - 128 * q else "ab"

    def legendre(qs, first, count):
        kinds = [kind_of(q, first) for q in qs]
        lane = lax.broadcasted_iota(jnp.int32, (16, 128), 1)
        sub = lax.broadcasted_iota(jnp.int32, (16, 128), 0)

        def block(p0):
            rows = pl.ds(p0, 16)
            acc = [[jnp.zeros((16, 128), F32) for _ in range(2)] for _ in qs]
            front = [128 * q + lane < K - p0 - sub for q in qs]
            for jj in range(ROWS):
                cols = pl.ds(128 * jj, 128)
                ca = cb = None
                if "a" in kinds or "ab" in kinds:
                    ca = [coef_a[part, rows, cols] for part in range(2)]
                if "b" in kinds or "ab" in kinds or "x" in kinds:
                    cb = [coef_b[part, rows, cols] for part in range(2)]
                for n, (q, kind) in enumerate(zip(qs, kinds)):
                    if kind == "x":
                        tt = t[jj, rows, K : K + 1].astype(F32)
                    else:
                        tt = t[jj, rows, 128 * q : 128 * q + 128].astype(F32)
                    for part in range(2):
                        if kind == "a":
                            c = ca[part]
                        elif kind == "ab":
                            c = jnp.where(front[n], ca[part], cb[part])
                        else:
                            c = cb[part]
                        acc[n][part] = acc[n][part] + c * tt
            for n, (q, kind) in enumerate(zip(qs, kinds)):
                if kind == "x":
                    both = jnp.where(lane < LAST[1], acc[n][0], acc[n][1])
                    place = 128 * PLACE[None, q]
                    partial[rows, place : place + 128] = both.astype(BF16)
                else:
                    for part in range(2):
                        place = 128 * PLACE[part, q]
                        partial[rows, place : place + 128] = acc[n][part].astype(BF16)

        def body(i, carry):
            for n in range(2):
                block(pl.multiple_of((first + 2 * i + n) * 16, 16))
            return carry

        lax.fori_loop(0, count // 2, body, 0)

    def sums_of(*qs):
        first = 0
        for block in range(1, HK // 16 + 1):
            if block == HK // 16 or any(
                kind_of(q, block) != kind_of(q, first) for q in qs
            ):
                legendre(qs, first, block - first)
                first = block

    core_copy, x_copy, z_copy = {}, {}, {}
    offset = START

    def core_step(c):
        n = 128 * len(CHUNKS[c])
        cols = slice(offset[c], offset[c] + n)
        mine = partial[:, cols]
        core_send[:, cols] = jnp.dot(
            onehot[pl.ds(0, 160), :], mine, preferred_element_type=F32
        ).astype(BF16)
        core_copy[c] = pltpu.make_async_remote_copy(
            src_ref=core_send.at[:, cols],
            dst_ref=core_recv.at[:, cols],
            send_sem=core_sem.at[0, c],
            recv_sem=core_sem.at[1, c],
            device_id=core_peer,
            device_id_type=mesh_id,
        )
        core_copy[c].start()
        own[:, cols] = jnp.dot(
            onehot[pl.ds(160, 160), :], mine, preferred_element_type=F32
        )

    def x_step(c):
        n = 128 * len(CHUNKS[c])
        cols = slice(offset[c], offset[c] + n)
        core_copy[c].wait_recv()
        x_send[:, cols] = (
            own[pl.ds(0, 80), cols] + core_recv[pl.ds(0, 80), cols].astype(F32)
        ).astype(BF16)
        x_copy[c] = pltpu.make_async_remote_copy(
            src_ref=x_send.at[:, cols],
            dst_ref=x_recv.at[:, cols],
            send_sem=x_sem.at[0, c],
            recv_sem=x_sem.at[1, c],
            device_id=x_peer,
            device_id_type=mesh_id,
        )
        x_copy[c].start()

    def z_step(c):
        n = 128 * len(CHUNKS[c])
        cols = slice(offset[c], offset[c] + n)
        x_copy[c].wait_recv()
        summed[:, cols] = (
            own[pl.ds(80, 80), cols]
            + core_recv[pl.ds(80, 80), cols].astype(F32)
            + x_recv[:, cols].astype(F32)
        )
        for d in range(NZ):
            for i in range(len(CHUNKS[c])):
                packed[c, d, 5 * i : 5 * i + 5, :] = summed[
                    5 * d : 5 * d + 5, offset[c] + 128 * i : offset[c] + 128 * i + 128
                ]
        for d in range(1, NZ):
            z_send[c, d] = packed[c, d].astype(BF16)
        if c == 0:
            heard(4, 5)
        z_copy[c] = []
        for d in ZORDER:
            copy = pltpu.make_async_remote_copy(
                src_ref=z_send.at[c, d],
                dst_ref=z_recv.at[c, d],
                send_sem=zs_sem.at[c, d],
                recv_sem=zr_sem.at[c, d],
                device_id=z_peer[d],
                device_id_type=mesh_id,
            )
            copy.start()
            z_copy[c].append(copy)

    sums_of(0, 1)
    core_step(0)
    sums_of(2)
    core_step(1)
    x_step(0)
    sums_of(3)
    core_step(2)
    x_step(1)
    sums_of(4, 5)
    core_step(3)
    x_step(2)
    z_step(0)
    x_step(3)
    z_step(1)
    z_step(2)
    z_step(3)

    thickness = thick[0]
    for copy in halo_copy:
        copy.wait_send()
    for c in range(len(CHUNKS)):
        for copy in z_copy[c]:
            copy.wait_recv()
        total = packed[c, 0]
        for d in range(1, NZ):
            total = total + z_recv[c, d].astype(F32)
        field[0, pl.ds(ZROWS * c, ZROWS), :] = total
        lev_send[pl.ds(ZROWS * c, ZROWS), :] = (total * thickness).astype(BF16)
    lev_copy = {
        d: pltpu.make_async_remote_copy(
            src_ref=lev_send,
            dst_ref=lev_recv.at[d],
            send_sem=ls_sem.at[d],
            recv_sem=lr_sem.at[d],
            device_id=lev_peer[d],
            device_id_type=mesh_id,
        )
        for d in range(1, 8)
    }
    for d in range(7, 0, -1):

        @pl.when(lev >= d)
        def _():
            lev_copy[d].start()

    field[1] = (0.5 * thickness) * field[0]
    for d in range(1, 8):

        @pl.when(lev + d < 8)
        def _():
            lev_copy[d].wait_recv()
            field[1] += lev_recv[d].astype(F32)

    save.wait()
    for c in range(len(CHUNKS)):
        core_copy[c].wait_send()
        x_copy[c].wait_send()
        for copy in z_copy[c]:
            copy.wait_send()
    for d in range(1, 8):

        @pl.when(lev >= d)
        def _():
            lev_copy[d].wait_send()


def finish(smooth_in, field, smooth_out, spectral, sem):
    copy = pltpu.make_async_copy(smooth_in, smooth_out, sem)
    copy.start()
    for f in range(2):
        for c, tiles in enumerate(CHUNKS):
            for n, (part, q) in enumerate(tiles):
                for i in range(SLOTS):
                    k = ZROWS * c + 5 * n + i
                    if part is None:
                        for half in range(2):
                            spectral[f, i, half : half + 1, K : K + 1] = field[
                                f, k : k + 1, LAST[half] : LAST[half] + 1
                            ]
                    else:
                        spectral[f, i, part : part + 1, 128 * q : 128 * q + 128] = (
                            field[f, k : k + 1, :]
                        )
    copy.wait()


def on_device(air, kappa, thick, table, perm):
    vmem = pl.BlockSpec(memory_space=pltpu.VMEM)
    hbm = pl.BlockSpec(memory_space=pl.ANY)
    nc = len(CHUNKS)
    wide = 128 * TILES
    grid = jax.ShapeDtypeStruct((1, 2, ROWS, LON), BF16)
    smooth, field = pl.pallas_call(
        kernel,
        out_shape=(grid, jax.ShapeDtypeStruct((2, nc * ZROWS, 128), F32)),
        in_specs=[hbm, hbm, pl.BlockSpec(memory_space=pltpu.SMEM), hbm, hbm, hbm, hbm],
        out_specs=(hbm, vmem),
        scratch_shapes=[
            pltpu.VMEM((1, 2, ROWS, LON), BF16),
            pltpu.VMEM((2, ROWS, LON), BF16),
            pltpu.VMEM((HK,), jnp.int32),
            pltpu.VMEM((1, 2, ROWS, LON), BF16),
            pltpu.VMEM((2, 16, 512), F32),
            pltpu.VMEM((2, 16, 512), BF16),
            pltpu.VMEM((2, 16, 512), BF16),
            pltpu.VMEM((2, ROWS, LON), F32),
            pltpu.VMEM((2, ROWS, LON), F32),
            pltpu.VMEM((4 * HK, WAVE), BF16),
            pltpu.VMEM((128, ROWS * 128), BF16),
            pltpu.VMEM((ROWS, HK, K + 1), BF16),
            pltpu.VMEM((64, WAVE), BF16),
            pltpu.VMEM((64, WAVE), BF16),
            pltpu.VMEM((HK, HK), BF16),
            pltpu.VMEM((2, HK, ROWS * 128), F32),
            pltpu.VMEM((2, HK, ROWS * 128), F32),
            pltpu.VMEM((HK, wide), BF16),
            pltpu.VMEM((160, wide), BF16),
            pltpu.VMEM((160, wide), BF16),
            pltpu.VMEM((160, wide), F32),
            pltpu.VMEM((80, wide), BF16),
            pltpu.VMEM((80, wide), BF16),
            pltpu.VMEM((80, wide), F32),
            pltpu.VMEM((nc, NZ, ZROWS, 128), F32),
            pltpu.VMEM((nc, NZ, ZROWS, 128), BF16),
            pltpu.VMEM((nc, NZ, ZROWS, 128), BF16),
            pltpu.VMEM((nc * ZROWS, 128), BF16),
            pltpu.VMEM((8, nc * ZROWS, 128), BF16),
            pltpu.SemaphoreType.DMA((8 + ROWS,)),
            pltpu.SemaphoreType.DMA,
            pltpu.SemaphoreType.DMA((2, 2)),
            pltpu.SemaphoreType.DMA((2, nc)),
            pltpu.SemaphoreType.DMA((2, nc)),
            pltpu.SemaphoreType.DMA((nc, NZ)),
            pltpu.SemaphoreType.DMA((nc, NZ)),
            pltpu.SemaphoreType.DMA((8,)),
            pltpu.SemaphoreType.DMA((8,)),
            pltpu.SemaphoreType.REGULAR((9,)),
        ],
        compiler_params=pltpu.CompilerParams(
            collective_id=0, has_side_effects=True, vmem_limit_bytes=56 * 2**20
        ),
        name="transform",
    )(
        air,
        kappa,
        thick,
        perm,
        jnp.asarray(fourier_table()),
        jnp.asarray(spread_tables()),
        table,
    )
    smooth, spectral = pl.pallas_call(
        finish,
        out_shape=(grid, jax.ShapeDtypeStruct((2, SLOTS, 2, K + 1), F32)),
        in_specs=[vmem, vmem],
        out_specs=(hbm, vmem),
        scratch_shapes=[pltpu.SemaphoreType.DMA],
        name="finish",
    )(smooth, field)
    return smooth, jnp.transpose(spectral, (0, 2, 1, 3))[None]


def solution(mesh):
    return jax.shard_map(
        on_device,
        mesh=mesh,
        in_specs=(
            P("lev", None, "band", None),
            P(None, "band", None),
            P("lev"),
            P("band", None, None),
            P(),
        ),
        out_specs=(P("lev", None, "band", None), P("lev", None, None, "band", None)),
        check_vma=False,
    )
```

time: 63.5 us -> 50.3 us (0.79)
  the two profiles are of different devices: /device:TPU:1 before, /device:TPU:2 now
where the time goes in v2:
time: 50.3 us; the launch traced here: 50.1 us
  Pallas kernels  48.8 us (97%)
  between operations  1.28 us (3%)
    pallas_call x1, Pallas kernels, on_device(): pl.pallas_call(kernel, out_shape=(grid, jax.ShapeDtypeStruct((2, nc * ZRO...  46.6 us
    pallas_call x1, Pallas kernels, on_device(): pl.pallas_call(finish, out_shape=(grid, jax.ShapeDtypeStruct((2, SLOTS, 2...  2.19 us

profile of v2, /device:TPU:2, one launch (start us, length us, event | category | flops | bytes accessed | tf_op | source)
XLA Modules:
  0.0 50.1 jit_solution(15342425874117048750)
XLA Ops:
  1.3 46.6 %transform.1 = (bf16[1,2,8,4096]{3,2,1,0:T(8,128)(2,1)}, f32[2,64,128]{2,1,0:T(8,128)}) custom-call(bf16[1,2,8,4096]{3,2,1,0:T(8,128)(2,1)} %air_hbm.1, bf16[2,8,4096]{2,1,0:T(8,128)(2,1)} %kappa_hbm.1, f32[1]{0:T(128)S(6)} %copy.9.thick, s32[320]{0:T(512)} %perm_hbm.1, bf16[1280,1024]{1,0:T(8,128)(2,1)} %constant.4.clone.w_hbm, ...), custom_call_target="tpu_custom_call" | custom-call | tf_op jit(solution)/shard_map/transform/pallas_call | solution.py:467
  47.9 2.2 %finish.1 = (bf16[1,2,8,4096]{3,2,1,0:T(8,128)(2,1)}, f32[2,5,2,641]{3,2,1,0:T(2,128)}) custom-call(bf16[1,2,8,4096]{3,2,1,0:T(8,128)(2,1)} %get-tuple-element.6.smooth_in, f32[2,64,128]{2,1,0:T(8,128)} %get-tuple-element.7.field), custom_call_target="tpu_custom_call" | custom-call | tf_op jit(solution)/shard_map/finish/pallas_call | solution.py:526

commit v3 on v2

--- a/solution.py
+++ b/solution.py
@@ -30,8 +30,8 @@
 START = tuple(128 * PLACE[c[0]] for c in CHUNKS)
 ZROWS = 16
 TILES = len(PLACE)
-LAST = (0, 2)
-ZORDER = (8, 7, 9, 6, 10, 5, 11, 4, 12, 3, 13, 2, 14, 1, 15)
+LAST = 1
+ZORDER = (4, 3, 5, 2, 6, 1, 7)
 
 
 def fourier_table():
@@ -59,13 +59,13 @@
 
 
 def kernel(
-    air_hbm, kappa_hbm, thick, perm_hbm, w_hbm, e_hbm, t_hbm,
+    air_hbm, kappa_hbm, thick_hbm, perm_hbm, w_hbm, e_hbm, t_hbm,
     smooth_hbm, field,
-    air, kappa, perm, smooth,
-    halo_rows, halo_send, halo_recv, base, x_base, w, e, t, xc, xs, onehot, coef_a, coef_b, partial,
-    core_send, core_recv, own, x_send, x_recv, summed, packed, z_send, z_recv,
+    air, kappa, thick, perm, smooth,
+    halo_rows, halo_send, halo_recv, base, x_base, w, e, t, xc, xs, onehot, coef, partial,
+    core_send, core_recv, own, kept, quad_send, quad_recv, summed, packed, z_send, z_recv,
     lev_send, lev_recv,
-    in_sem, out_sem, halo_sem, core_sem, x_sem, zs_sem, zr_sem, ls_sem, lr_sem, told,
+    in_sem, out_sem, halo_sem, core_sem, qs_sem, qr_sem, zs_sem, zr_sem, ls_sem, lr_sem, told,
 ):
     band = lax.axis_index("band")
     lev = lax.axis_index("lev")
@@ -76,7 +76,12 @@
 
     yy, xhi = lev // 2, lev % 2
     core_peer = at(z, xlo, 1 - core, lev)
-    x_peer = at(z, 1 - xlo, core, lev)
+    pair_z = z + 1 - 2 * (z % 2)
+    quad_peer = (
+        at(pair_z, 1 - xlo, core, lev),
+        at(z, 1 - xlo, core, lev),
+        at(pair_z, xlo, core, lev),
+    )
     z_peer = {d: at((z + d) % NZ, xlo, core, lev) for d in range(1, NZ)}
     lev_peer = {d: at(z, xlo, core, (lev + 8 - d) % 8) for d in range(1, 8)}
     y_peer = {d: at(z, xlo, core, ((yy + d) % 4) * 2 + xhi) for d in (1, 3)}
@@ -86,7 +91,7 @@
 
     barrier = pltpu.get_barrier_semaphore()
     peers = [
-        *halo_peer, x_peer, z_peer[1], z_peer[15], y_peer[1], y_peer[3], far_x_peer,
+        *halo_peer, *quad_peer, z_peer[2], z_peer[14], y_peer[1], y_peer[3], far_x_peer,
     ]
     for peer in peers:
         pl.semaphore_signal(barrier, inc=1, device_id=peer, device_id_type=mesh_id)
@@ -109,6 +114,7 @@
                 for k in (0, 2, 1, 3)
             ]
             + [(e_hbm, e)]
+            + [(thick_hbm, thick)]
             + [(t_hbm.at[k], t.at[k]) for k in range(ROWS)]
         )
     ]
@@ -141,10 +147,10 @@
     ]
     for copy in halo_copy:
         copy.start()
-    tell(0, z_peer[1])
-    tell(1, z_peer[15])
-    tell(6, y_peer[1])
-    tell(7, y_peer[3])
+    tell(0, z_peer[2])
+    tell(1, z_peer[14])
+    tell(5, y_peer[1])
+    tell(6, y_peer[3])
     j = (band * ROWS + row).astype(F32)
     step = math.pi / STEPS
     centre = jnp.sin((j + 0.5) * step)
@@ -168,18 +174,19 @@
     r = lax.broadcasted_iota(jnp.int32, (HK, HK), 0)
     col = lax.broadcasted_iota(jnp.int32, (HK, HK), 1)
     group = (r * 205) >> 10
-    dz, dx, dc = group & 15, (group >> 4) & 1, group >> 5
+    dz, dp, dx, dc = group & 7, (group >> 3) & 1, (group >> 4) & 1, group >> 5
+    to_z = (jnp.where(dp == 0, pair_z, z) + 2 * dz) & 15
     to_x = jnp.where(dx == 0, 1 - xlo, xlo)
     to_c = jnp.where(dc == 0, 1 - core, core)
-    slot = ((((z + dz) & 15) * 2 + to_x) * 2 + to_c) * SLOTS + (r - 5 * group)
+    slot = ((to_z * 2 + to_x) * 2 + to_c) * SLOTS + (r - 5 * group)
     order = jnp.where(slot == col, 1.0, 0.0).astype(BF16)
     pair_of = jnp.where(r == perm[...].reshape(1, HK), 1.0, 0.0).astype(BF16)
     onehot[...] = nt(order, pair_of).astype(BF16)
 
-    heard(0, 1, 6, 7)
-    tell(2, z_peer[2])
-    tell(3, z_peer[14])
-    tell(8, far_x_peer)
+    heard(0, 1, 5, 6)
+    tell(2, z_peer[4])
+    tell(3, z_peer[12])
+    tell(4, far_x_peer)
 
     folded = []
     for way in range(2):
@@ -215,27 +222,29 @@
     pairs = lax.broadcasted_iota(jnp.int32, (HK, 64), 0)
     group = lax.broadcasted_iota(jnp.int32, (HK, 64), 1) >> 4
     loads[7].wait()
-    for back in range(2):
-        m = (K - 1 - pairs if back else pairs) & 3
-        loads[3 + 2 * back].wait()
-        loads[4 + 2 * back].wait()
-        cosine = nt(w[pl.ds(back * HK, HK), :], xc[...])
-        sine = nt(w[pl.ds(K + back * HK, HK), :], xs[...])
-        target = coef_b if back else coef_a
+    def fourier(back, carry):
+        m = jnp.where(back == 1, K - 1 - pairs, pairs) & 3
+        for k in range(2):
+            pltpu.make_async_copy(
+                w_hbm.at[pl.ds(0, HK)], w.at[pl.ds(0, HK)], in_sem.at[3 + 2 * back + k]
+            ).wait()
+        first = pl.multiple_of(back * HK, HK)
+        cosine = nt(w[pl.ds(first, HK), :], xc[...])
+        sine = nt(w[pl.ds(K + first, HK), :], xs[...])
         turn = jnp.where(m == 1, 1.0, -1.0)
         real = cosine + jnp.where(group == 2, turn * sine, 0.0)
         imag = sine - jnp.where(group == 3, turn * cosine, 0.0)
         odd = (m & 1) == 1
         for part, (f, g) in enumerate(((real, 2), (imag, 3))):
             keep = group == jnp.where(odd, g, m >> 1)
-            target[part] = jnp.dot(
+            coef[back, part] = jnp.dot(
                 jnp.where(keep, f, 0.0).astype(BF16),
-                e[pl.ds(64 * back, 64), :],
+                e[pl.ds(pl.multiple_of(64 * back, 64), 64), :],
                 preferred_element_type=F32,
             )
-    heard(2, 3, 8)
-    tell(4, z_peer[4])
-    tell(5, z_peer[12])
+        return carry
+
+    lax.fori_loop(0, 2, fourier, 0)
     for load in loads[8:]:
         load.wait()
 
@@ -253,15 +262,15 @@
 
         def block(p0):
             rows = pl.ds(p0, 16)
-            acc = [[jnp.zeros((16, 128), F32) for _ in range(2)] for _ in qs]
+            acc = [[0.0, 0.0] for _ in qs]
             front = [128 * q + lane < K - p0 - sub for q in qs]
             for jj in range(ROWS):
                 cols = pl.ds(128 * jj, 128)
                 ca = cb = None
                 if "a" in kinds or "ab" in kinds:
-                    ca = [coef_a[part, rows, cols] for part in range(2)]
+                    ca = [coef[0, part, rows, cols] for part in range(2)]
                 if "b" in kinds or "ab" in kinds or "x" in kinds:
-                    cb = [coef_b[part, rows, cols] for part in range(2)]
+                    cb = [coef[1, part, rows, cols] for part in range(2)]
                 for n, (q, kind) in enumerate(zip(qs, kinds)):
                     if kind == "x":
                         tt = t[jj, rows, K : K + 1].astype(F32)
@@ -272,12 +281,14 @@
                             c = ca[part]
                         elif kind == "ab":
                             c = jnp.where(front[n], ca[part], cb[part])
+                        elif kind == "b":
+                            c = cb[part]
                         else:
-                            c = cb[part]
+                            c = cb[part][:, :1]
                         acc[n][part] = acc[n][part] + c * tt
             for n, (q, kind) in enumerate(zip(qs, kinds)):
                 if kind == "x":
-                    both = jnp.where(lane < LAST[1], acc[n][0], acc[n][1])
+                    both = jnp.where(lane < LAST, acc[n][0], acc[n][1])
                     place = 128 * PLACE[None, q]
                     partial[rows, place : place + 128] = both.astype(BF16)
                 else:
@@ -301,7 +312,7 @@
                 legendre(qs, first, block - first)
                 first = block
 
-    core_copy, x_copy, z_copy = {}, {}, {}
+    core_copy, quad_copy, z_copy = {}, {}, {}
     offset = START
 
     def core_step(c):
@@ -324,49 +335,59 @@
             onehot[pl.ds(160, 160), :], mine, preferred_element_type=F32
         )
 
-    def x_step(c):
-        n = 128 * len(CHUNKS[c])
-        cols = slice(offset[c], offset[c] + n)
+    def quad_step(c):
+        count = len(CHUNKS[c])
+        cols = slice(offset[c], offset[c] + 128 * count)
         core_copy[c].wait_recv()
-        x_send[:, cols] = (
-            own[pl.ds(0, 80), cols] + core_recv[pl.ds(0, 80), cols].astype(F32)
-        ).astype(BF16)
-        x_copy[c] = pltpu.make_async_remote_copy(
-            src_ref=x_send.at[:, cols],
-            dst_ref=x_recv.at[:, cols],
-            send_sem=x_sem.at[0, c],
-            recv_sem=x_sem.at[1, c],
-            device_id=x_peer,
-            device_id_type=mesh_id,
-        )
-        x_copy[c].start()
+        both = own[:, cols] + core_recv[:, cols].astype(F32)
+        parts = [
+            [both[40 * g : 40 * g + 40, 128 * n : 128 * n + 128] for n in range(count)]
+            for g in range(4)
+        ]
+        quad_copy[c] = []
+        for g in range(3):
+            pad = [] if count == 2 else [jnp.zeros((8, 128), F32)]
+            rows = pl.ds(0, 40 * count + 8 * len(pad))
+            quad_send[c, g, rows, :] = jnp.concatenate(parts[g] + pad, axis=0).astype(
+                BF16
+            )
+            copy = pltpu.make_async_remote_copy(
+                src_ref=quad_send.at[c, g, rows],
+                dst_ref=quad_recv.at[c, g, rows],
+                send_sem=qs_sem.at[c, g],
+                recv_sem=qr_sem.at[c, g],
+                device_id=quad_peer[g],
+                device_id_type=mesh_id,
+            )
+            copy.start()
+            quad_copy[c].append(copy)
+        kept[c, pl.ds(0, 40 * count), :] = jnp.concatenate(parts[3], axis=0)
 
     def z_step(c):
-        n = 128 * len(CHUNKS[c])
-        cols = slice(offset[c], offset[c] + n)
-        x_copy[c].wait_recv()
-        summed[:, cols] = (
-            own[pl.ds(80, 80), cols]
-            + core_recv[pl.ds(80, 80), cols].astype(F32)
-            + x_recv[:, cols].astype(F32)
-        )
-        for d in range(NZ):
-            for i in range(len(CHUNKS[c])):
-                packed[c, d, 5 * i : 5 * i + 5, :] = summed[
-                    5 * d : 5 * d + 5, offset[c] + 128 * i : offset[c] + 128 * i + 128
+        count = len(CHUNKS[c])
+        rows = 40 * count
+        total = kept[c, pl.ds(0, rows), :]
+        size = rows + (8 if count == 3 else 0)
+        for g in range(3):
+            quad_copy[c][g].wait_recv()
+            total = total + quad_recv[c, g, pl.ds(0, size), :].astype(F32)[:rows, :]
+        summed[c, pl.ds(0, rows), :] = total
+        for d in range(NZ // 2):
+            for n in range(count):
+                packed[c, d, 5 * n : 5 * n + 5, :] = summed[
+                    c, 40 * n + 5 * d : 40 * n + 5 * d + 5, :
                 ]
-        for d in range(1, NZ):
-            z_send[c, d] = packed[c, d].astype(BF16)
         if c == 0:
-            heard(4, 5)
+            heard(2, 3, 4)
         z_copy[c] = []
         for d in ZORDER:
+            z_send[c, d] = packed[c, d].astype(BF16)
             copy = pltpu.make_async_remote_copy(
                 src_ref=z_send.at[c, d],
                 dst_ref=z_recv.at[c, d],
                 send_sem=zs_sem.at[c, d],
                 recv_sem=zr_sem.at[c, d],
-                device_id=z_peer[d],
+                device_id=z_peer[2 * d],
                 device_id_type=mesh_id,
             )
             copy.start()
@@ -376,66 +397,71 @@
     core_step(0)
     sums_of(2)
     core_step(1)
-    x_step(0)
+    quad_step(0)
     sums_of(3)
     core_step(2)
-    x_step(1)
+    quad_step(1)
     sums_of(4, 5)
     core_step(3)
-    x_step(2)
+    quad_step(2)
+    quad_step(3)
     z_step(0)
-    x_step(3)
     z_step(1)
     z_step(2)
     z_step(3)
 
-    thickness = thick[0]
+    thickness = thick[...].reshape(1, 1)
     for copy in halo_copy:
         copy.wait_send()
+    half = len(CHUNKS) // 2 * ZROWS
+    lev_copy = {}
     for c in range(len(CHUNKS)):
         for copy in z_copy[c]:
             copy.wait_recv()
         total = packed[c, 0]
-        for d in range(1, NZ):
+        for d in range(1, NZ // 2):
             total = total + z_recv[c, d].astype(F32)
-        field[0, pl.ds(ZROWS * c, ZROWS), :] = total
-        lev_send[pl.ds(ZROWS * c, ZROWS), :] = (total * thickness).astype(BF16)
-    lev_copy = {
-        d: pltpu.make_async_remote_copy(
-            src_ref=lev_send,
-            dst_ref=lev_recv.at[d],
-            send_sem=ls_sem.at[d],
-            recv_sem=lr_sem.at[d],
-            device_id=lev_peer[d],
-            device_id_type=mesh_id,
-        )
-        for d in range(1, 8)
-    }
-    for d in range(7, 0, -1):
-
-        @pl.when(lev >= d)
-        def _():
-            lev_copy[d].start()
-
-    field[1] = (0.5 * thickness) * field[0]
+        rows = pl.ds(ZROWS * c, ZROWS)
+        total_w = total * thickness
+        lev_send[rows, :] = total_w.astype(BF16)
+        field[0, rows, :] = total
+        field[1, rows, :] = 0.5 * total_w
+        if c % 2:
+            h = c // 2
+            part = pl.ds(half * h, half)
+            for d in range(7, 0, -1):
+                lev_copy[h, d] = pltpu.make_async_remote_copy(
+                    src_ref=lev_send.at[part],
+                    dst_ref=lev_recv.at[d, part],
+                    send_sem=ls_sem.at[h, d],
+                    recv_sem=lr_sem.at[h, d],
+                    device_id=lev_peer[d],
+                    device_id_type=mesh_id,
+                )
+
+                @pl.when(lev >= d)
+                def _():
+                    lev_copy[h, d].start()
+
     for d in range(1, 8):
 
         @pl.when(lev + d < 8)
         def _():
-            lev_copy[d].wait_recv()
+            lev_copy[0, d].wait_recv()
+            lev_copy[1, d].wait_recv()
             field[1] += lev_recv[d].astype(F32)
 
     save.wait()
     for c in range(len(CHUNKS)):
         core_copy[c].wait_send()
-        x_copy[c].wait_send()
-        for copy in z_copy[c]:
+        for copy in quad_copy[c] + z_copy[c]:
             copy.wait_send()
     for d in range(1, 8):
 
         @pl.when(lev >= d)
         def _():
-            lev_copy[d].wait_send()
+            lev_copy[0, d].wait_send()
+            lev_copy[1, d].wait_send()
 
 
 def finish(smooth_in, field, smooth_out, spectral, sem):
@@ -449,7 +475,7 @@
                     if part is None:
                         for half in range(2):
                             spectral[f, i, half : half + 1, K : K + 1] = field[
-                                f, k : k + 1, LAST[half] : LAST[half] + 1
+                                f, k : k + 1, LAST * half : LAST * half + 1
                             ]
                     else:
                         spectral[f, i, part : part + 1, 128 * q : 128 * q + 128] = (
@@ -467,11 +493,12 @@
     smooth, field = pl.pallas_call(
         kernel,
         out_shape=(grid, jax.ShapeDtypeStruct((2, nc * ZROWS, 128), F32)),
-        in_specs=[hbm, hbm, pl.BlockSpec(memory_space=pltpu.SMEM), hbm, hbm, hbm, hbm],
+        in_specs=[hbm] * 7,
         out_specs=(hbm, vmem),
         scratch_shapes=[
             pltpu.VMEM((1, 2, ROWS, LON), BF16),
             pltpu.VMEM((2, ROWS, LON), BF16),
+            pltpu.VMEM((1,), F32),
             pltpu.VMEM((HK,), jnp.int32),
             pltpu.VMEM((1, 2, ROWS, LON), BF16),
             pltpu.VMEM((2, 16, 512), F32),
@@ -485,30 +512,31 @@
             pltpu.VMEM((64, WAVE), BF16),
             pltpu.VMEM((64, WAVE), BF16),
             pltpu.VMEM((HK, HK), BF16),
-            pltpu.VMEM((2, HK, ROWS * 128), F32),
-            pltpu.VMEM((2, HK, ROWS * 128), F32),
+            pltpu.VMEM((2, 2, HK, ROWS * 128), F32),
             pltpu.VMEM((HK, wide), BF16),
             pltpu.VMEM((160, wide), BF16),
             pltpu.VMEM((160, wide), BF16),
             pltpu.VMEM((160, wide), F32),
-            pltpu.VMEM((80, wide), BF16),
-            pltpu.VMEM((80, wide), BF16),
-            pltpu.VMEM((80, wide), F32),
-            pltpu.VMEM((nc, NZ, ZROWS, 128), F32),
-            pltpu.VMEM((nc, NZ, ZROWS, 128), BF16),
-            pltpu.VMEM((nc, NZ, ZROWS, 128), BF16),
+            pltpu.VMEM((nc, 128, 128), F32),
+            pltpu.VMEM((nc, 3, 128, 128), BF16),
+            pltpu.VMEM((nc, 3, 128, 128), BF16),
+            pltpu.VMEM((nc, 128, 128), F32),
+            pltpu.VMEM((nc, NZ // 2, ZROWS, 128), F32),
+            pltpu.VMEM((nc, NZ // 2, ZROWS, 128), BF16),
+            pltpu.VMEM((nc, NZ // 2, ZROWS, 128), BF16),
             pltpu.VMEM((nc * ZROWS, 128), BF16),
             pltpu.VMEM((8, nc * ZROWS, 128), BF16),
-            pltpu.SemaphoreType.DMA((8 + ROWS,)),
+            pltpu.SemaphoreType.DMA((9 + ROWS,)),
             pltpu.SemaphoreType.DMA,
             pltpu.SemaphoreType.DMA((2, 2)),
             pltpu.SemaphoreType.DMA((2, nc)),
-            pltpu.SemaphoreType.DMA((2, nc)),
-            pltpu.SemaphoreType.DMA((nc, NZ)),
-            pltpu.SemaphoreType.DMA((nc, NZ)),
-            pltpu.SemaphoreType.DMA((8,)),
-            pltpu.SemaphoreType.DMA((8,)),
-            pltpu.SemaphoreType.REGULAR((9,)),
+            pltpu.SemaphoreType.DMA((nc, 3)),
+            pltpu.SemaphoreType.DMA((nc, 3)),
+            pltpu.SemaphoreType.DMA((nc, NZ // 2)),
+            pltpu.SemaphoreType.DMA((nc, NZ // 2)),
+            pltpu.SemaphoreType.DMA((2, 8)),
+            pltpu.SemaphoreType.DMA((2, 8)),
+            pltpu.SemaphoreType.REGULAR((7,)),
         ],
         compiler_params=pltpu.CompilerParams(
             collective_id=0, has_side_effects=True, vmem_limit_bytes=56 * 2**20

time: 50.3 us -> 46.6 us (0.926)
  the two profiles are of different devices: /device:TPU:2 before, /device:TPU:1 now
where the time goes in v3:
time: 46.6 us; the launch traced here: 46.4 us
  Pallas kernels  45.2 us (97%)
  between operations  1.28 us (3%)
    pallas_call x1, Pallas kernels, on_device(): pl.pallas_call(kernel, out_shape=(grid, jax.ShapeDtypeStruct((2, nc * ZRO...  43 us
    pallas_call x1, Pallas kernels, on_device(): pl.pallas_call(finish, out_shape=(grid, jax.ShapeDtypeStruct((2, SLOTS, 2...  2.19 us

profile of v3, /device:TPU:1, one launch (start us, length us, event | category | flops | bytes accessed | tf_op | source)
XLA Modules:
  0.0 46.4 jit_solution(5988850350158678042)
XLA Ops:
  1.3 43.0 %transform.1 = (bf16[1,2,8,4096]{3,2,1,0:T(8,128)(2,1)}, f32[2,64,128]{2,1,0:T(8,128)}) custom-call(bf16[1,2,8,4096]{3,2,1,0:T(8,128)(2,1)} %air_hbm.1, bf16[2,8,4096]{2,1,0:T(8,128)(2,1)} %kappa_hbm.1, f32[1]{0:T(128)S(6)} %copy.9.thick_hbm, s32[320]{0:T(512)} %perm_hbm.1, bf16[1280,1024]{1,0:T(8,128)(2,1)} %constant.4.clone.w_hbm, ...), custom_call_target="tpu_custom_call" | custom-call | tf_op jit(solution)/shard_map/transform/pallas_call | solution.py:493
  44.2 2.2 %finish.1 = (bf16[1,2,8,4096]{3,2,1,0:T(8,128)(2,1)}, f32[2,5,2,641]{3,2,1,0:T(2,128)}) custom-call(bf16[1,2,8,4096]{3,2,1,0:T(8,128)(2,1)} %get-tuple-element.6.smooth_in, f32[2,64,128]{2,1,0:T(8,128)} %get-tuple-element.7.field), custom_call_target="tpu_custom_call" | custom-call | tf_op jit(solution)/shard_map/finish/pallas_call | solution.py:554

commit v4 on v3

--- a/solution.py
+++ b/solution.py
@@ -31,7 +31,8 @@
 ZROWS = 16
 TILES = len(PLACE)
 LAST = 1
-ZORDER = (4, 3, 5, 2, 6, 1, 7)
+FAR = (4, 3, 5)
+NEAR = (2, 6, 1, 7)
 
 
 def fourier_table():
@@ -379,9 +380,13 @@
                 ]
         if c == 0:
             heard(2, 3, 4)
+        for d in range(1, NZ // 2):
+            z_send[c, d] = packed[c, d].astype(BF16)
         z_copy[c] = []
-        for d in ZORDER:
-            z_send[c, d] = packed[c, d].astype(BF16)
+        send_z(c, FAR)
+
+    def send_z(c, steps):
+        for d in steps:
             copy = pltpu.make_async_remote_copy(
                 src_ref=z_send.at[c, d],
                 dst_ref=z_recv.at[c, d],
@@ -409,6 +414,8 @@
     z_step(1)
     z_step(2)
     z_step(3)
+    for c in range(len(CHUNKS)):
+        send_z(c, NEAR)
 
     thickness = thick[...].reshape(1, 1)
     for copy in halo_copy:

time: 46.6 us -> 45.5 us (0.976)
  Pallas kernels: 45.2 us -> 44.1 us
    pallas_call x1, Pallas kernels: 43 us -> 41.9 us  [on_device(): pl.pallas_call(kernel, out_shape=(grid, jax.ShapeDtypeStruct((2, nc * ZRO...]
where the time goes in v4:
time: 45.5 us; the launch traced here: 45.4 us
  Pallas kernels  44.1 us (97%)
  between operations  1.28 us (3%)
    pallas_call x1, Pallas kernels, on_device(): pl.pallas_call(kernel, out_shape=(grid, jax.ShapeDtypeStruct((2, nc * ZRO...  41.9 us
    pallas_call x1, Pallas kernels, on_device(): pl.pallas_call(finish, out_shape=(grid, jax.ShapeDtypeStruct((2, SLOTS, 2...  2.19 us

profile of v4, /device:TPU:1, one launch (start us, length us, event | category | flops | bytes accessed | tf_op | source)
XLA Modules:
  0.0 45.4 jit_solution(17638777100393301360)
XLA Ops:
  1.3 41.9 %transform.1 = (bf16[1,2,8,4096]{3,2,1,0:T(8,128)(2,1)}, f32[2,64,128]{2,1,0:T(8,128)}) custom-call(bf16[1,2,8,4096]{3,2,1,0:T(8,128)(2,1)} %air_hbm.1, bf16[2,8,4096]{2,1,0:T(8,128)(2,1)} %kappa_hbm.1, f32[1]{0:T(128)S(6)} %copy.9.thick_hbm, s32[320]{0:T(512)} %perm_hbm.1, bf16[1280,1024]{1,0:T(8,128)(2,1)} %constant.4.clone.w_hbm, ...), custom_call_target="tpu_custom_call" | custom-call | tf_op jit(solution)/shard_map/transform/pallas_call | solution.py:500
  43.2 2.2 %finish.1 = (bf16[1,2,8,4096]{3,2,1,0:T(8,128)(2,1)}, f32[2,5,2,641]{3,2,1,0:T(2,128)}) custom-call(bf16[1,2,8,4096]{3,2,1,0:T(8,128)(2,1)} %get-tuple-element.6.smooth_in, f32[2,64,128]{2,1,0:T(8,128)} %get-tuple-element.7.field), custom_call_target="tpu_custom_call" | custom-call | tf_op jit(solution)/shard_map/finish/pallas_call | solution.py:561

commit v5 on v4

--- a/solution.py
+++ b/solution.py
@@ -23,8 +23,8 @@
 CHUNKS = (
     ((0, 0), (1, 0), (0, 1)),
     ((1, 1), (0, 2), (1, 2)),
-    ((0, 3), (1, 3)),
-    ((0, 4), (1, 4), (None, 5)),
+    ((0, 3), (1, 3), (None, 5)),
+    ((0, 4), (1, 4)),
 )
 PLACE = {tile: k for k, tile in enumerate(t for c in CHUNKS for t in c)}
 START = tuple(128 * PLACE[c[0]] for c in CHUNKS)
@@ -336,6 +336,10 @@
             onehot[pl.ds(160, 160), :], mine, preferred_element_type=F32
         )
 
+    def turned(tile):
+        pad = jnp.zeros((128 - tile.shape[0], 128), F32)
+        return jnp.transpose(jnp.concatenate([tile, pad], axis=0))
+
     def quad_step(c):
         count = len(CHUNKS[c])
         cols = slice(offset[c], offset[c] + 128 * count)
@@ -347,11 +351,14 @@
         ]
         quad_copy[c] = []
         for g in range(3):
-            pad = [] if count == 2 else [jnp.zeros((8, 128), F32)]
-            rows = pl.ds(0, 40 * count + 8 * len(pad))
-            quad_send[c, g, rows, :] = jnp.concatenate(parts[g] + pad, axis=0).astype(
-                BF16
-            )
+            tiles = list(parts[g])
+            if CHUNKS[c][-1][0] is None:
+                tiles[-1] = turned(tiles[-1])[:8, :]
+            if count == 3:
+                tiles.append(jnp.zeros((8, 128), F32))
+            tiles = jnp.concatenate(tiles, axis=0)
+            rows = pl.ds(0, tiles.shape[0])
+            quad_send[c, g, rows, :] = tiles.astype(BF16)
             copy = pltpu.make_async_remote_copy(
                 src_ref=quad_send.at[c, g, rows],
                 dst_ref=quad_recv.at[c, g, rows],
@@ -367,12 +374,15 @@
     def z_step(c):
         count = len(CHUNKS[c])
         rows = 40 * count
-        total = kept[c, pl.ds(0, rows), :]
-        size = rows + (8 if count == 3 else 0)
+        thin = CHUNKS[c][-1][0] is None
+        size = 96 if thin else rows + (8 if count == 3 else 0)
+        came = 0.0
         for g in range(3):
             quad_copy[c][g].wait_recv()
-            total = total + quad_recv[c, g, pl.ds(0, size), :].astype(F32)[:rows, :]
-        summed[c, pl.ds(0, rows), :] = total
+            came = came + quad_recv[c, g, pl.ds(0, size), :].astype(F32)
+        if thin:
+            came = jnp.concatenate([came[:80], turned(came[80:88])[:40]], axis=0)
+        summed[c, pl.ds(0, rows), :] = kept[c, pl.ds(0, rows), :] + came[:rows]
         for d in range(NZ // 2):
             for n in range(count):
                 packed[c, d, 5 * n : 5 * n + 5, :] = summed[
@@ -403,10 +413,10 @@
     sums_of(2)
     core_step(1)
     quad_step(0)
-    sums_of(3)
+    sums_of(3, 5)
     core_step(2)
     quad_step(1)
-    sums_of(4, 5)
+    sums_of(4)
     core_step(3)
     quad_step(2)
     quad_step(3)
@@ -420,7 +430,7 @@
     thickness = thick[...].reshape(1, 1)
     for copy in halo_copy:
         copy.wait_send()
-    half = len(CHUNKS) // 2 * ZROWS
+    ends = len(CHUNKS) - 2, len(CHUNKS) - 1
     lev_copy = {}
     for c in range(len(CHUNKS)):
         for copy in z_copy[c]:
@@ -433,9 +443,9 @@
         lev_send[rows, :] = total_w.astype(BF16)
         field[0, rows, :] = total
         field[1, rows, :] = 0.5 * total_w
-        if c % 2:
-            h = c // 2
-            part = pl.ds(half * h, half)
+        if c in ends:
+            h = ends.index(c)
+            part = pl.ds(ZROWS * c, ZROWS) if h else pl.ds(0, ZROWS * (c + 1))
             for d in range(7, 0, -1):
                 lev_copy[h, d] = pltpu.make_async_remote_copy(
                     src_ref=lev_send.at[part],

time: 45.5 us -> 45.7 us (level)
  the two profiles are of different devices: /device:TPU:1 before, /device:TPU:32 now
where the time goes in v5:
time: 45.7 us; the launch traced here: 45.5 us
  Pallas kernels  44.2 us (97%)
  between operations  1.28 us (3%)
    pallas_call x1, Pallas kernels, on_device(): pl.pallas_call(kernel, out_shape=(grid, jax.ShapeDtypeStruct((2, nc * ZRO...  42 us
    pallas_call x1, Pallas kernels, on_device(): pl.pallas_call(finish, out_shape=(grid, jax.ShapeDtypeStruct((2, SLOTS, 2...  2.19 us

profile of v5, /device:TPU:32, one launch (start us, length us, event | category | flops | bytes accessed | tf_op | source)
XLA Modules:
  0.0 45.5 jit_solution(2277283749306299626)
XLA Ops:
  1.3 42.0 %transform.1 = (bf16[1,2,8,4096]{3,2,1,0:T(8,128)(2,1)}, f32[2,64,128]{2,1,0:T(8,128)}) custom-call(bf16[1,2,8,4096]{3,2,1,0:T(8,128)(2,1)} %air_hbm.1, bf16[2,8,4096]{2,1,0:T(8,128)(2,1)} %kappa_hbm.1, f32[1]{0:T(128)S(6)} %copy.9.thick_hbm, s32[320]{0:T(512)} %perm_hbm.1, bf16[1280,1024]{1,0:T(8,128)(2,1)} %constant.4.clone.w_hbm, ...), custom_call_target="tpu_custom_call" | custom-call | tf_op jit(solution)/shard_map/transform/pallas_call | solution.py:510
  43.3 2.2 %finish.1 = (bf16[1,2,8,4096]{3,2,1,0:T(8,128)(2,1)}, f32[2,5,2,641]{3,2,1,0:T(2,128)}) custom-call(bf16[1,2,8,4096]{3,2,1,0:T(8,128)(2,1)} %get-tuple-element.6.smooth_in, f32[2,64,128]{2,1,0:T(8,128)} %get-tuple-element.7.field), custom_call_target="tpu_custom_call" | custom-call | tf_op jit(solution)/shard_map/finish/pallas_call | solution.py:571
